TPU v7x, 128 devices: a whole 4x4x4 slice. The times are simulated.
128 devices in a mesh: shard: 8 (over z_hi, x), rep: 16 (over y, z_lo, core).
Axes of the slice: x: 4, y: 4, z: 4 (z_hi: 2, z_lo: 2; z = z_hi * 2 + z_lo), core: 2. Of those that a mesh axis runs over, the one named last changes fastest.
Arguments:
- latents: bfloat16 [1024, 256, 384], P(('shard', 'rep')), may hold values from -6 to 6
- conditions: bfloat16 [1024, 384], P(('shard', 'rep')), may hold values from -6 to 6
- counts: int32 [128], P(('shard', 'rep')), may hold values from 0 to 8, as said below
- mod_weight: bfloat16 [384, 2304], P('shard'), may hold values from -0.3125 to 0.3125
- mod_bias: bfloat16 [2304], P('shard'), may hold values from -3 to 3
- qkv_weight: bfloat16 [384, 1152], P('shard'), may hold values from -0.3125 to 0.3125
- qv_bias: bfloat16 [768], P('shard'), may hold values from -3 to 3
- proj_weight: bfloat16 [384, 384], P('shard'), may hold values from -1.25 to 1.25
- proj_bias: bfloat16 [384], P('shard'), may hold values from -3 to 3
- up_weight: bfloat16 [384, 1536], P('shard'), may hold values from -0.3125 to 0.3125
- up_bias: bfloat16 [1536], P('shard'), may hold values from -3 to 3
- down_weight: bfloat16 [1536, 384], P('shard'), may hold values from -0.15625 to 0.15625
- down_bias: bfloat16 [384], P('shard'), may hold values from -3 to 3
- grad_out: bfloat16 [1024, 256, 384], P(('shard', 'rep')), may hold values from -6 to 6
Outputs:
- output: bfloat16 [1024, 256, 384], P(('shard', 'rep'))
- grad_latents: bfloat16 [1024, 256, 384], P(('shard', 'rep'))
- grad_conditions: bfloat16 [1024, 384], P(('shard', 'rep'))
- grad_mod_weight: float32 [384, 2304], P('shard')
- grad_mod_bias: float32 [2304], P('shard')
- grad_qkv_weight: float32 [384, 1152], P('shard')
- grad_qv_bias: float32 [768], P('shard')
- grad_proj_weight: float32 [384, 384], P('shard')
- grad_proj_bias: float32 [384], P('shard')
- grad_up_weight: float32 [384, 1536], P('shard')
- grad_up_bias: float32 [1536], P('shard')
- grad_down_weight: float32 [1536, 384], P('shard')
- grad_down_bias: float32 [384], P('shard')
Inputs may be any that keep to these rules, and one draw needn't show every extreme that they name: Device d (shard index slowest, then rep) holds its latents in its first counts[d] of 8 slots; the other slots are padding. Some device holds 8 latents and some holds none.
All inputs are finite; a program needn't handle non-finite values.
Results may differ from a plain program's by a relative error of at most 0.023.
Values may be sent and summed in bfloat16 or wider, within the bound.
No kernel may reach another device: no remote copies, remote signals or barrier semaphores. Data moves between devices by JAX's collectives and lax.ppermute only.
A program may use at most 192 MiB of HBM per device.

v0:
```python
import jax
import jax.numpy as jnp
from jax import lax
from jax.sharding import PartitionSpec as P

HEADS = 6
HEAD_DIM = 64


def normalize(value):
    center = jnp.mean(value, axis=-1, keepdims=True)
    centered = value - center
    spread = jnp.mean(centered * centered, axis=-1, keepdims=True)
    inverse = lax.rsqrt(spread + 1e-06)
    return (centered * inverse, inverse)


def norm_back(grad, normed, inverse):
    first = jnp.mean(grad, axis=-1, keepdims=True)
    second = jnp.mean(grad * normed, axis=-1, keepdims=True)
    return inverse * (grad - first - normed * second)


def product(left, right):
    return jnp.dot(left, right, preferred_element_type=jnp.float32)


def outer_sum(left, right):
    return lax.dot_general(
        left, right, (((0,), (0,)), ((), ())), preferred_element_type=jnp.float32
    )


def back_product(left, right):
    return lax.dot_general(
        left, right, (((1,), (1,)), ((), ())), preferred_element_type=jnp.float32
    )


def on_device(
    latents,
    conditions,
    counts,
    mod_weight,
    mod_bias,
    qkv_weight,
    qv_bias,
    proj_weight,
    proj_bias,
    up_weight,
    up_bias,
    down_weight,
    down_bias,
    grad_out,
):
    slots, length, width = latents.shape
    heads = HEADS
    head_dim = HEAD_DIM
    rows = slots * length
    factor = head_dim ** (-0.5)
    valid = (jnp.arange(slots) < counts[0]).astype(jnp.float32)[:, None, None]
    gathered = (
        lax.all_gather(mod_weight, "shard", axis=0, tiled=True),
        lax.all_gather(mod_bias, "shard", axis=0, tiled=True),
        lax.all_gather(qkv_weight, "shard", axis=0, tiled=True),
        lax.all_gather(qv_bias, "shard", axis=0, tiled=True),
        lax.all_gather(proj_weight, "shard", axis=0, tiled=True),
        lax.all_gather(proj_bias, "shard", axis=0, tiled=True),
        lax.all_gather(up_weight, "shard", axis=0, tiled=True),
        lax.all_gather(up_bias, "shard", axis=0, tiled=True),
        lax.all_gather(down_weight, "shard", axis=0, tiled=True),
        lax.all_gather(down_bias, "shard", axis=0, tiled=True),
    )
    (
        mod_full,
        mod_bias_full,
        qkv_full,
        qv_bias_full,
        proj_full,
        proj_bias_full,
        up_full,
        up_bias_full,
        down_full,
        down_bias_full,
    ) = gathered
    cond_float = conditions.astype(jnp.float32)
    cond_act, silu_pull = jax.vjp(jax.nn.silu, cond_float)
    cond_low = cond_act.astype(jnp.bfloat16)
    modulation = product(cond_low, mod_full) + mod_bias_full.astype(jnp.float32)
    pieces = jnp.split(modulation, 6, axis=-1)
    shift_one, scale_one, gate_one, shift_two, scale_two, gate_two = [
        piece[:, None, :] for piece in pieces
    ]
    inputs = latents.astype(jnp.float32)
    normed_one, inverse_one = normalize(inputs)
    hidden_one = (
        (normed_one * (1.0 + scale_one) + shift_one).astype(jnp.bfloat16).reshape(rows, width)
    )
    qv_float = qv_bias_full.astype(jnp.float32)
    full_bias = jnp.concatenate(
        [qv_float[:width], jnp.zeros((width,), jnp.float32), qv_float[width:]]
    )
    qkv_low = (product(hidden_one, qkv_full) + full_bias).astype(jnp.bfloat16)
    qkv_heads = qkv_low.reshape(slots, length, 3, heads, head_dim)
    queries = qkv_heads[:, :, 0]
    keys = qkv_heads[:, :, 1]
    values = qkv_heads[:, :, 2]
    scores = (
        jnp.einsum("lqhd,lkhd->lhqk", queries, keys, preferred_element_type=jnp.float32) * factor
    )
    top = jnp.max(scores, axis=-1, keepdims=True)
    expo = jnp.exp(scores - top)
    total = jnp.sum(expo, axis=-1, keepdims=True)
    logsum = top + jnp.log(total)
    probs_low = (expo / total).astype(jnp.bfloat16)
    mixed = jnp.einsum("lhqk,lkhd->lqhd", probs_low, values, preferred_element_type=jnp.float32)
    mixed_low = mixed.astype(jnp.bfloat16).reshape(rows, width)
    branch_one = (product(mixed_low, proj_full) + proj_bias_full.astype(jnp.float32)).reshape(
        slots, length, width
    )
    middle = inputs + gate_one * branch_one
    normed_two, inverse_two = normalize(middle)
    hidden_two = (
        (normed_two * (1.0 + scale_two) + shift_two).astype(jnp.bfloat16).reshape(rows, width)
    )
    upward = product(hidden_two, up_full) + up_bias_full.astype(jnp.float32)
    activated, gelu_pull = jax.vjp(lambda value: jax.nn.gelu(value, approximate=True), upward)
    act_low = activated.astype(jnp.bfloat16)
    branch_two = (product(act_low, down_full) + down_bias_full.astype(jnp.float32)).reshape(
        slots, length, width
    )
    output = ((middle + gate_two * branch_two) * valid).astype(jnp.bfloat16)
    again = (
        lax.all_gather(mod_weight, "shard", axis=0, tiled=True),
        lax.all_gather(qkv_weight, "shard", axis=0, tiled=True),
        lax.all_gather(proj_weight, "shard", axis=0, tiled=True),
        lax.all_gather(up_weight, "shard", axis=0, tiled=True),
        lax.all_gather(down_weight, "shard", axis=0, tiled=True),
    )
    mod_back, qkv_back, proj_back, up_back, down_back = again
    cotangent = grad_out.astype(jnp.float32) * valid
    grad_gate_two = jnp.sum(cotangent * branch_two, axis=1)
    grad_branch_two = (cotangent * gate_two).astype(jnp.bfloat16).reshape(rows, width)
    grad_down = outer_sum(act_low, grad_branch_two)
    grad_down_bias = jnp.sum(grad_branch_two.astype(jnp.float32), axis=0)
    grad_act = back_product(grad_branch_two, down_back)
    (grad_up_raw,) = gelu_pull(grad_act)
    grad_upward = grad_up_raw.astype(jnp.bfloat16)
    grad_up = outer_sum(hidden_two, grad_upward)
    grad_up_bias = jnp.sum(grad_upward.astype(jnp.float32), axis=0)
    grad_hidden_two = back_product(grad_upward, up_back).reshape(slots, length, width)
    grad_shift_two = jnp.sum(grad_hidden_two, axis=1)
    grad_scale_two = jnp.sum(grad_hidden_two * normed_two, axis=1)
    grad_middle = cotangent + norm_back(
        grad_hidden_two * (1.0 + scale_two), normed_two, inverse_two
    )
    grad_gate_one = jnp.sum(grad_middle * branch_one, axis=1)
    grad_branch_one = (grad_middle * gate_one).astype(jnp.bfloat16).reshape(rows, width)
    grad_proj = outer_sum(mixed_low, grad_branch_one)
    grad_proj_bias = jnp.sum(grad_branch_one.astype(jnp.float32), axis=0)
    grad_mixed = (
        back_product(grad_branch_one, proj_back)
        .astype(jnp.bfloat16)
        .reshape(slots, length, heads, head_dim)
    )
    scores_again = (
        jnp.einsum("lqhd,lkhd->lhqk", queries, keys, preferred_element_type=jnp.float32) * factor
    )
    probs_full = jnp.exp(scores_again - logsum)
    probs_back = probs_full.astype(jnp.bfloat16)
    grad_values = jnp.einsum(
        "lhqk,lqhd->lkhd", probs_back, grad_mixed, preferred_element_type=jnp.float32
    )
    grad_probs = jnp.einsum(
        "lqhd,lkhd->lhqk", grad_mixed, values, preferred_element_type=jnp.float32
    )
    grad_scores = (
        probs_full * (grad_probs - jnp.sum(probs_full * grad_probs, axis=-1, keepdims=True))
    ).astype(jnp.bfloat16)
    grad_queries = (
        jnp.einsum("lhqk,lkhd->lqhd", grad_scores, keys, preferred_element_type=jnp.float32)
        * factor
    )
    grad_keys = (
        jnp.einsum("lhqk,lqhd->lkhd", grad_scores, queries, preferred_element_type=jnp.float32)
        * factor
    )
    grad_qkv = (
        jnp.stack([grad_queries, grad_keys, grad_values], axis=2)
        .astype(jnp.bfloat16)
        .reshape(rows, 3 * width)
    )
    grad_qkv_full = outer_sum(hidden_one, grad_qkv)
    bias_sums = jnp.sum(grad_qkv.astype(jnp.float32), axis=0)
    grad_qv = jnp.concatenate([bias_sums[:width], bias_sums[2 * width :]])
    grad_hidden_one = back_product(grad_qkv, qkv_back).reshape(slots, length, width)
    grad_shift_one = jnp.sum(grad_hidden_one, axis=1)
    grad_scale_one = jnp.sum(grad_hidden_one * normed_one, axis=1)
    grad_inputs = grad_middle + norm_back(
        grad_hidden_one * (1.0 + scale_one), normed_one, inverse_one
    )
    grad_mod = jnp.concatenate(
        [
            grad_shift_one,
            grad_scale_one,
            grad_gate_one,
            grad_shift_two,
            grad_scale_two,
            grad_gate_two,
        ],
        axis=-1,
    ).astype(jnp.bfloat16)
    grad_mod_full = outer_sum(cond_low, grad_mod)
    grad_mod_bias = jnp.sum(grad_mod.astype(jnp.float32), axis=0)
    grad_cond_act = back_product(grad_mod, mod_back)
    (grad_cond,) = silu_pull(grad_cond_act)
    owned = (
        lax.psum_scatter(
            grad_mod_full.astype(jnp.bfloat16), "shard", scatter_dimension=0, tiled=True
        ).astype(jnp.float32),
        lax.psum_scatter(
            grad_mod_bias.astype(jnp.bfloat16), "shard", scatter_dimension=0, tiled=True
        ).astype(jnp.float32),
        lax.psum_scatter(
            grad_qkv_full.astype(jnp.bfloat16), "shard", scatter_dimension=0, tiled=True
        ).astype(jnp.float32),
        lax.psum_scatter(
            grad_qv.astype(jnp.bfloat16), "shard", scatter_dimension=0, tiled=True
        ).astype(jnp.float32),
        lax.psum_scatter(
            grad_proj.astype(jnp.bfloat16), "shard", scatter_dimension=0, tiled=True
        ).astype(jnp.float32),
        lax.psum_scatter(
            grad_proj_bias.astype(jnp.bfloat16), "shard", scatter_dimension=0, tiled=True
        ).astype(jnp.float32),
        lax.psum_scatter(
            grad_up.astype(jnp.bfloat16), "shard", scatter_dimension=0, tiled=True
        ).astype(jnp.float32),
        lax.psum_scatter(
            grad_up_bias.astype(jnp.bfloat16), "shard", scatter_dimension=0, tiled=True
        ).astype(jnp.float32),
        lax.psum_scatter(
            grad_down.astype(jnp.bfloat16), "shard", scatter_dimension=0, tiled=True
        ).astype(jnp.float32),
        lax.psum_scatter(
            grad_down_bias.astype(jnp.bfloat16), "shard", scatter_dimension=0, tiled=True
        ).astype(jnp.float32),
    )
    summed = (
        lax.psum(owned[0].astype(jnp.bfloat16), "rep").astype(jnp.float32),
        lax.psum(owned[1].astype(jnp.bfloat16), "rep").astype(jnp.float32),
        lax.psum(owned[2].astype(jnp.bfloat16), "rep").astype(jnp.float32),
        lax.psum(owned[3].astype(jnp.bfloat16), "rep").astype(jnp.float32),
        lax.psum(owned[4].astype(jnp.bfloat16), "rep").astype(jnp.float32),
        lax.psum(owned[5].astype(jnp.bfloat16), "rep").astype(jnp.float32),
        lax.psum(owned[6].astype(jnp.bfloat16), "rep").astype(jnp.float32),
        lax.psum(owned[7].astype(jnp.bfloat16), "rep").astype(jnp.float32),
        lax.psum(owned[8].astype(jnp.bfloat16), "rep").astype(jnp.float32),
        lax.psum(owned[9].astype(jnp.bfloat16), "rep").astype(jnp.float32),
    )
    return (
        output,
        grad_inputs.astype(jnp.bfloat16),
        grad_cond.astype(jnp.bfloat16),
        summed[0],
        summed[1],
        summed[2],
        summed[3],
        summed[4],
        summed[5],
        summed[6],
        summed[7],
        summed[8],
        summed[9],
    )


def solution(mesh):
    in_specs = (
        P(("shard", "rep"), None, None),
        P(("shard", "rep"), None),
        P(("shard", "rep")),
        P("shard", None),
        P("shard"),
        P("shard", None),
        P("shard"),
        P("shard", None),
        P("shard"),
        P("shard", None),
        P("shard"),
        P("shard", None),
        P("shard"),
        P(("shard", "rep"), None, None),
    )
    out_specs = (
        P(("shard", "rep"), None, None),
        P(("shard", "rep"), None, None),
        P(("shard", "rep"), None),
        P("shard", None),
        P("shard"),
        P("shard", None),
        P("shard"),
        P("shard", None),
        P("shard"),
        P("shard", None),
        P("shard"),
        P("shard", None),
        P("shard"),
    )
    return jax.shard_map(
        on_device, mesh=mesh, in_specs=in_specs, out_specs=out_specs, check_vma=False
    )
```

profile of v0, /device:TPU:1, one launch (start us, length us, event | category | flops | bytes accessed | tf_op | source)
XLA Modules:
  0.0 765.8 jit_solution(3501092138588833403)
XLA Ops:
  18.8 36.4 %all-reduce.13 = (bf16[2304]{0:T(1024)(128)(2,1)S(1)}, bf16[768]{0:T(1024)(128)(2,1)S(1)}, bf16[384]{0:T(512)(128)(2,1)S(1)}, bf16[1536]{0:T(1024)(128)(2,1)S(1)}, bf16[384]{0:T(512)(128)(2,1)S(1)}) all-reduce(bf16[2304]{0:T(1024)(128)(2,1)S(1)} %dynamic-update-slice, ...), channel_id=1, replica_groups=mesh['shard'=8,'rep'=16] {'shard'}, use_global_device_ids=true, to_apply=%add | all-reduce | flops 5376 | bytes 21504
  58.6 28.3 %all_gather.39 = bf16[384,384]{1,0:T(8,128)(2,1)S(1)} all-gather(bf16[48,384]{1,0:T(8,128)(2,1)S(1)} %copy-done.44), channel_id=1, replica_groups=mesh['shard'=8,'rep'=16] {'shard'}, dimensions={0}, use_global_device_ids=true | all-gather | bytes 331776 | tf_op jit(solution)/shard_map/all_gather | solution.py:67
  86.8 33.3 %all_gather.37 = bf16[384,1152]{1,0:T(8,128)(2,1)} all-gather(bf16[48,1152]{1,0:T(8,128)(2,1)S(1)} %copy-done.36), channel_id=1, replica_groups=mesh['shard'=8,'rep'=16] {'shard'}, dimensions={0}, use_global_device_ids=true | all-gather | bytes 995328 | tf_op jit(solution)/shard_map/all_gather | solution.py:65
  128.0 6.7 copy.66
  134.7 4.4 copy.89
  159.0 11.0 %multiply_convert_fusion.1 = (bf16[2048,1536]{1,0:T(8,128)(2,1)}, f32[2048,1536]{1,0:T(8,128)}) fusion(f32[1536]{0:T(1024)S(1)} %convert_element_type.191, bf16[2048,384]{1,0:T(8,128)(2,1)} %bitcast.135, bf16[384,1536]{1,0:T(8,128)(2,1)} %all-gather.6.cloned.1.call-done), kind=kOutput, calls=%fused_computation.12 | convolution fusion | flops 2447376384 | bytes 21633024 | tf_op jit(solution)/shard_map/dot_general | solution.py:25
  169.9 15.1 %fusion.63 = (bf16[1536]{0:T(1024)(128)(2,1)}, bf16[2048,1536]{1,0:T(8,128)(2,1)S(1)}) fusion(f32[2048,1536]{1,0:T(8,128)} %get-tuple-element.71, f32[1536]{0:T(1024)S(1)} %convert_element_type.191, bf16[2048,384]{1,0:T(8,128)(2,1)} %bitcast.133, bf16[1536,384]{1,0:T(8,128)(2,1)} %all-gather.8.cloned.1.call-done), kind=kOutput, calls=%fused_computation.125 | convolution fusion | flops 2485123584 | bytes 21636096 | tf_op jit(solution)/shard_map/dot_general | solution.py:35
  185.0 5.1 fusion.30
  190.7 6.0 convolution_add_fusion.3
  208.4 7.2 fusion.32
  215.6 9.1 %multiply_reduce_fusion = (f32[8,6,256]{2,1,0:T(8,128)S(1)}, f32[8,6,256,256]{2,3,1,0:T(8,128)}) fusion(f32[8,6,256,256]{2,3,1,0:T(8,128)} %copy-done, f32[8,6,256]{2,1,0:T(8,128)S(1)} %log_add_fusion, bf16[8,256,1,6,64]{1,0,4,3,2:T(8,128)(2,1)S(1)} %copy-done.19, bf16[8,256,6,64]{1,0,3,2:T(8,128)(2,1)S(1)} %bitcast.122), kind=kOutput, calls=%fused_computation.10 | convolution fusion | flops 415223808 | bytes 28409856 | tf_op jit(solution)/shard_map/lqhd,lkhd->lhqk/dot_general | solution.py:174
  224.7 7.1 multiply_convert_fusion
  245.0 6.4 convolution_convert_fusion.4
  251.8 5.3 copy.78
  257.1 7.4 convolution_convert_fusion.3
  264.7 6.5 fusion.28
  279.6 49.6 %reduce-scatter.8.cloned.1.call-done = bf16[48,1152]{1,0:T(8,128)(2,1)} async-done(((bf16[384,1152]{1,0:T(8,128)(2,1)}), bf16[48,1152]{1,0:T(8,128)(2,1)}) %reduce-scatter.8.cloned.1.call-update) | async-done | bytes 110608 | tf_op jit(solution)/shard_map/reduce_scatter | solution.py:224
  329.2 76.3 %reduce-scatter.12.cloned.1.call-done = bf16[48,1536]{1,0:T(8,128)(2,1)} async-done(((bf16[384,1536]{1,0:T(8,128)(2,1)}), bf16[48,1536]{1,0:T(8,128)(2,1)}) %reduce-scatter.12.cloned.1.call-update) | async-done | bytes 147472 | tf_op jit(solution)/shard_map/reduce_scatter | solution.py:236
  405.5 75.9 %reduce-scatter.14.cloned.1.call-done = bf16[192,384]{1,0:T(8,128)(2,1)} async-done(((bf16[1536,384]{1,0:T(8,128)(2,1)}), bf16[192,384]{1,0:T(8,128)(2,1)}) %reduce-scatter.14.cloned.1.call-update) | async-done | bytes 147472 | tf_op jit(solution)/shard_map/reduce_scatter | solution.py:242
  481.4 78.8 %reduce-scatter.6.cloned.1.call-done = bf16[48,2304]{1,0:T(8,128)(2,1)} async-done(((bf16[384,2304]{1,0:T(8,128)(2,1)}), bf16[48,2304]{1,0:T(8,128)(2,1)}) %reduce-scatter.6.cloned.1.call-update) | async-done | bytes 221200 | tf_op jit(solution)/shard_map/reduce_scatter | solution.py:218
  563.1 31.7 %all-reduce.12 = (bf16[2304]{0:T(1024)(128)(2,1)S(1)}, bf16[768]{0:T(1024)(128)(2,1)S(1)}, bf16[384]{0:T(512)(128)(2,1)S(1)}, bf16[1536]{0:T(1024)(128)(2,1)S(1)}, bf16[384]{0:T(512)(128)(2,1)S(1)}) all-reduce(bf16[2304]{0:T(1024)(128)(2,1)S(1)} %reduce_sum.217, ...), channel_id=3, replica_groups=mesh['shard'=8,'rep'=16] {'shard'}, use_global_device_ids=true, to_apply=%region_20.21.clone | all-reduce | flops 5376 | bytes 21504
  596.4 33.8 %reduce-scatter.10.cloned.1.call-done = bf16[48,384]{1,0:T(8,128)(2,1)} async-done(((bf16[384,384]{1,0:T(8,128)(2,1)}), bf16[48,384]{1,0:T(8,128)(2,1)}) %reduce-scatter.10.cloned.1.call-update) | async-done | bytes 36880 | tf_op jit(solution)/shard_map/reduce_scatter | solution.py:230
  630.1 52.0 %all-reduce.10 = (bf16[288]{0:T(512)(128)(2,1)S(1)}, bf16[96]{0:T(256)(128)(2,1)S(1)}, bf16[48,384]{1,0:T(8,128)(2,1)S(1)}, bf16[48]{0:T(256)(128)(2,1)S(1)}, bf...) all-reduce(bf16[288]{0:T(512)(128)(2,1)S(1)} %dynamic-slice.6, ...), channel_id=1, replica_groups=mesh['shard'=8,'rep'=16] {'rep'}, use_global_device_ids=true, to_apply=%region_21.22 | all-reduce | flops 19104 | bytes 76416 | tf_op jit(solution)/shard_map/psum | solution.py:251
  685.5 66.9 %all-reduce.16.cloned.1.call-done = (bf16[48,2304]{1,0:T(8,128)(2,1)}, bf16[48,1152]{1,0:T(8,128)(2,1)}, bf16[48,1536]{1,0:T(8,128)(2,1)}, bf16[192,384]{1,0:T(8,128)(2,1)}) async-done(((bf16[48,2304]{1,0:T(8,128)(2,1)}, bf16[48,1152]{1,0:T(8,128)(2,1)}, bf16[48,1536]{1,0:T(8,128)(2,1)}, bf16[192,384]{1,0:T(8,128)(2,1)}), (bf16[48,2304]{1,0:T(8,128)(2,1)}, bf16[48,1152]{1,0:T(8,128)(2,1)}, ...) | async-done | bytes 626704 | tf_op jit(solution)/shard_map/psum | solution.py:250
  (220 shorter events, 84.6 us)
Async XLA Ops:
  7.2 50.4 %copy-start.5 = (bf16[8,256,384]{2,1,0:T(8,128)(2,1)S(1)}, bf16[8,256,384]{2,1,0:T(8,128)(2,1)}, u32[]{:S(2)}) copy-start(bf16[8,256,384]{2,1,0:T(8,128)(2,1)} %param.14) | copy-start | bytes 4718596
  7.2 51.3 %copy-start.44 = (bf16[48,384]{1,0:T(8,128)(2,1)S(1)}, bf16[48,384]{1,0:T(8,128)(2,1)}, u32[]{:S(2)}) copy-start(bf16[48,384]{1,0:T(8,128)(2,1)} %param.21) | copy-start | bytes 110596
  7.2 79.6 %copy-start.36 = (bf16[48,1152]{1,0:T(8,128)(2,1)S(1)}, bf16[48,1152]{1,0:T(8,128)(2,1)}, u32[]{:S(2)}) copy-start(bf16[48,1152]{1,0:T(8,128)(2,1)} %param.19) | copy-start | bytes 331780
  7.2 113.0 %copy-start.41 = (bf16[8,384]{1,0:T(8,128)(2,1)S(1)}, bf16[8,384]{1,0:T(8,128)(2,1)}, u32[]{:S(2)}) copy-start(bf16[8,384]{1,0:T(8,128)(2,1)} %param.15) | copy-start | bytes 18436
  7.2 113.0 %all-gather.4.cloned.1.call-start = ((), (), s32[]{:S(2)}) async-start(), calls=%async_computation.5 | async-start | bytes 1990656 | tf_op jit(solution)/shard_map/all_gather | solution.py:63
  8.0 151.0 %all-gather.6.cloned.1.call-start = ((), (), s32[]{:S(2)}) async-start(), calls=%async_computation.6 | async-start | bytes 1327104 | tf_op jit(solution)/shard_map/all_gather | solution.py:69
  8.7 161.2 %all-gather.8.cloned.1.call-start = ((), (), s32[]{:S(2)}) async-start(), calls=%async_computation.7 | async-start | bytes 1327104 | tf_op jit(solution)/shard_map/all_gather | solution.py:71
  9.4 319.7 %reduce-scatter.8.cloned.1.call-start = ((), (), s32[]{:S(2)}) async-start(), calls=%async_computation.9 | async-start | bytes 995328 | tf_op jit(solution)/shard_map/reduce_scatter | solution.py:224
  57.6 66.0 %copy-start.32 = (f32[8,256]{1,0:T(8,128)}, f32[8,256]{1,0:T(8,128)S(1)}, u32[]{:S(2)}) copy-start(f32[8,256]{1,0:T(8,128)S(1)} %broadcast_multiply_fusion.5) | copy-start | bytes 24580
  58.5 65.1 %copy-start.39 = (f32[8,256]{1,0:T(8,128)}, f32[8,256]{1,0:T(8,128)S(1)}, u32[]{:S(2)}) copy-start(f32[8,256]{1,0:T(8,128)S(1)} %add_rsqrt_fusion.1) | copy-start | bytes 24580
  169.9 15.1 %copy-start.26 = (bf16[384,1536]{1,0:T(8,128)(2,1)S(1)}, bf16[384,1536]{1,0:T(8,128)(2,1)}, u32[]{:S(2)}) copy-start(bf16[384,1536]{1,0:T(8,128)(2,1)} %all-gather.6.cloned.1.call-done) | copy-start | bytes 3538948
  208.4 16.3 %slice-start = ((s8[12582912]{0:T(1024)(128)(4,1)}), s8[4194304]{0:T(1024)(128)(4,1)S(1)}, s32[]{:S(2)}) async-start(s8[12582912]{0:T(1024)(128)(4,1)} %bitcast.114), calls=%async_computation.14 | async-start | bytes 8388608
  208.4 16.3 %slice-start.1 = ((s8[12582912]{0:T(1024)(128)(4,1)}), s8[4194304]{0:T(1024)(128)(4,1)S(1)}, s32[]{:S(2)}) async-start(s8[12582912]{0:T(1024)(128)(4,1)} %bitcast.114), calls=%async_computation.15 | async-start | bytes 8388608
  215.6 9.1 %slice-start.2 = ((s8[12582912]{0:T(1024)(128)(4,1)}), s8[4194304]{0:T(1024)(128)(4,1)S(1)}, s32[]{:S(2)}) async-start(s8[12582912]{0:T(1024)(128)(4,1)} %bitcast.114), calls=%async_computation.16 | async-start | bytes 8388608
  244.9 160.6 %reduce-scatter.12.cloned.1.call-start = ((), (), s32[]{:S(2)}) async-start(), calls=%async_computation.11 | async-start | bytes 1327104 | tf_op jit(solution)/shard_map/reduce_scatter | solution.py:236
  251.5 229.9 %reduce-scatter.14.cloned.1.call-start = ((), (), s32[]{:S(2)}) async-start(), calls=%async_computation.12 | async-start | bytes 1327104 | tf_op jit(solution)/shard_map/reduce_scatter | solution.py:242
  257.1 7.5 copy-start.40
  264.6 295.7 %reduce-scatter.6.cloned.1.call-start = ((), (), s32[]{:S(2)}) async-start(), calls=%async_computation.8 | async-start | bytes 1990656 | tf_op jit(solution)/shard_map/reduce_scatter | solution.py:218
  276.2 286.9 %copy-start.50 = (bf16[384]{0:T(512)(128)(2,1)S(1)}, bf16[384]{0:T(512)(128)(2,1)}, u32[]{:S(2)}) copy-start(bf16[384]{0:T(512)(128)(2,1)} %get-tuple-element.40) | copy-start | bytes 2308
  276.2 286.9 %copy-start.51 = (bf16[384]{0:T(512)(128)(2,1)S(1)}, bf16[384]{0:T(512)(128)(2,1)}, u32[]{:S(2)}) copy-start(bf16[384]{0:T(512)(128)(2,1)} %get-tuple-element.42) | copy-start | bytes 2308
  276.2 286.9 %copy-start.52 = (bf16[1536]{0:T(1024)(128)(2,1)S(1)}, bf16[1536]{0:T(1024)(128)(2,1)}, u32[]{:S(2)}) copy-start(bf16[1536]{0:T(1024)(128)(2,1)} %get-tuple-element.77) | copy-start | bytes 9220
  276.2 319.0 %copy-start.17 = (bf16[384,2304]{1,0:T(8,128)(2,1)S(1)}, bf16[384,2304]{1,0:T(8,128)(2,1)}, u32[]{:S(2)}) copy-start(bf16[384,2304]{1,0:T(8,128)(2,1)} %all-gather.4.cloned.1.call-done) | copy-start | bytes 5308420
  276.2 353.9 %reduce-scatter.10.cloned.1.call-start = ((), (), s32[]{:S(2)}) async-start(), calls=%async_computation.10 | async-start | bytes 331776 | tf_op jit(solution)/shard_map/reduce_scatter | solution.py:230
  279.5 472.9 %all-reduce.16.cloned.1.call-start = ((), (), s32[]{:S(2)}) async-start(), calls=%async_computation.13 | async-start | bytes 1253376 | tf_op jit(solution)/shard_map/psum | solution.py:250
  (41 other events, 162.5 us)
Sparse Core Ops, SparseCore 0:
  10.4 54.9 all-gather.3
  67.7 47.3 all-gather.5
  117.4 48.2 all-gather.7
  245.1 84.0 reduce-scatter.7
  333.2 72.2 reduce-scatter.11
  409.1 72.2 reduce-scatter.13
  485.7 74.5 reduce-scatter.5
  564.8 65.2 reduce-scatter.9
  632.9 119.4 all-reduce.15
where the time goes:
time: 770 us; the launch traced here: 766 us
  waiting for transfers between devices  383 us (50%)
  blocking collectives  182 us (24%)
  matrix products  100 us (13%)
  other arithmetic  42.1 us (5%)
  local copies, waits for them, and re-layouts  37 us (5%)
  between operations  20.8 us (3%)
    reduce_scatter x1, waiting for transfers between devices, on_device(): lax.psum_scatter(grad_mod_full.astype(jnp.bfloat16), 'shard', scatter_dim...  78.8 us
    reduce_scatter x1, waiting for transfers between devices, on_device(): lax.psum_scatter(grad_up.astype(jnp.bfloat16), 'shard', scatter_dimension...  76.3 us
    reduce_scatter x1, waiting for transfers between devices, on_device(): lax.psum_scatter(grad_down.astype(jnp.bfloat16), 'shard', scatter_dimensi...  75.9 us
    unnamed x2, blocking collectives  68.1 us
    psum x1, waiting for transfers between devices, on_device(): lax.psum(owned[0].astype(jnp.bfloat16), 'rep').astype(jnp.float32)  66.9 us
    psum x1, blocking collectives, on_device(): lax.psum(owned[1].astype(jnp.bfloat16), 'rep').astype(jnp.float32)  52 us
    reduce_scatter x1, waiting for transfers between devices, on_device(): lax.psum_scatter(grad_qkv_full.astype(jnp.bfloat16), 'shard', scatter_dim...  49.6 us
    reduce_scatter x1, waiting for transfers between devices, on_device(): lax.psum_scatter(grad_proj.astype(jnp.bfloat16), 'shard', scatter_dimensi...  33.8 us
  transfers between devices with their start and end apart: 9, of which 6 were waited for; matrix products, arithmetic and copies ran while one was open for 12% of the time, Pallas kernels for 0%

commit v1 on v0

v1 whole, which is shorter than its diff:
```python
import functools

import jax
import jax.numpy as jnp
from jax import lax
from jax.experimental import pallas as pl
from jax.experimental.pallas import tpu as pltpu
from jax.sharding import PartitionSpec as P

D = 384
HEADS = 6
HEAD_DIM = 64
FF = 1536
TOK = 256
CAP = 8
STEP = 1
TWIN = 128
BF = jnp.bfloat16
F32 = jnp.float32
VMEM_BYTES = 56 * 1024 * 1024

LANES_ONE = 2048
QKV_W = 3 * D
MOD_ONE = 2 * D
BIAS_ONE = QKV_W + MOD_ONE
LANES_TWO = 5120
MOD_TWO = 4 * D
AT_MOD = FF
AT_PROJ = AT_MOD + MOD_TWO
AT_DOWN = AT_PROJ + D
BIAS_TWO = AT_DOWN + FF
ROW_QKV, ROW_MOD, ROW_PROJ, ROW_UP, ROW_DOWN = 0, 9, 27, 30, 42


def dot(left, right):
    return jnp.dot(left, right, preferred_element_type=F32)


def dot_tn(left, right):
    return lax.dot_general(left, right, (((0,), (0,)), ((), ())), preferred_element_type=F32)


def dot_nt(left, right):
    return lax.dot_general(left, right, (((1,), (1,)), ((), ())), preferred_element_type=F32)


def normalize(value):
    center = jnp.mean(value, axis=-1, keepdims=True)
    centered = value - center
    spread = jnp.mean(centered * centered, axis=-1, keepdims=True)
    inverse = lax.rsqrt(spread + 1e-06)
    return centered * inverse, inverse


def norm_back(grad, normed, inverse):
    first = jnp.mean(grad, axis=-1, keepdims=True)
    second = jnp.mean(grad * normed, axis=-1, keepdims=True)
    return inverse * (grad - first - normed * second)


def bias_row(bias, first, count):
    return jnp.concatenate([bias[first + i : first + i + 1, :] for i in range(count)], axis=1)


def silu(cond):
    return cond * (1.0 / (1.0 + jnp.exp(-cond)))


def assemble(info, pieces, full):
    column, z_high, core = info[1], info[2], info[3]
    for k in range(4):
        spot = lax.rem(column + k, 4) * 48
        mine = (z_high ^ core) * 192 + spot
        other = (1 - (z_high ^ core)) * 192 + spot
        full[pl.ds(pl.multiple_of(mine, 16), 48), :] = pieces[k][...]
        full[pl.ds(pl.multiple_of(other, 16), 48), :] = pieces[4 + k][...]


def forward_kernel(
    info, latents, conditions, p0, p1, p2, p3, p4, p5, p6, p7,
    weights, bias_out, mod_out, qkv_out, expo_out, mixed_out, rinv_out, hidden_out,
):
    step = pl.program_id(0)

    @pl.when(step == 0)
    def _():
        assemble(info, (p0, p1, p2, p3, p4, p5, p6, p7), weights)
        total = jnp.zeros((48, 128), F32)
        for k in range(8):
            total += weights[48 * k : 48 * k + 48, BIAS_ONE : BIAS_ONE + 128].astype(F32)
        bias_out[...] = total
        cond_low = silu(conditions[...].astype(F32)).astype(BF)
        mod_out[...] = dot(cond_low, weights[:, QKV_W : QKV_W + MOD_ONE]) + bias_row(
            total, ROW_MOD, 6
        )

    @pl.when(step < info[0])
    def _():
        mod = mod_out[pl.ds(step, 1), :]
        normed, _ = normalize(latents[0].astype(F32))
        hidden = (normed * (1.0 + mod[:, D : 2 * D]) + mod[:, :D]).astype(BF)
        hidden_out[0] = hidden
        full_bias = bias_row(bias_out[0:16, :], ROW_QKV, 9)
        qkv = (dot(hidden, weights[:, :QKV_W]) + full_bias).astype(BF)
        qkv_out[0] = qkv
        low = lax.broadcasted_iota(jnp.int32, (TOK, 128), 1) < HEAD_DIM
        ones = jnp.ones((TOK, 128), BF)
        for pair in range(HEADS // 2):
            at = 128 * pair
            query = qkv[:, at : at + 128] * jnp.asarray(HEAD_DIM**-0.5, BF)
            key = qkv[:, D + at : D + at + 128]
            value = jnp.concatenate([qkv[:, 2 * D + at : 2 * D + at + 128], ones], axis=1)
            parts = []
            for half in range(2):
                chosen = jnp.where(low if half == 0 else ~low, query, jnp.zeros_like(query))
                scores = dot_nt(chosen, key)
                expo = jnp.exp(scores - jnp.max(scores, axis=-1, keepdims=True)).astype(BF)
                expo_out[0, 2 * pair + half] = expo
                parts.append(dot(expo, value))
            total = jnp.where(low, parts[0][:, 128:], parts[1][:, 128:])
            inverse = 1.0 / total
            rinv_out[0, :, at : at + 128] = inverse
            mixed_out[0, :, at : at + 128] = (
                jnp.where(low, parts[0][:, :128], parts[1][:, :128]) * inverse
            ).astype(BF)


def middle_kernel(
    info, latents, conditions, mixed_in, grad_out, bias_in, p0, p1, p2, p3, p4, p5, p6, p7,
    weights, out, grad_mid_out, grad_mixed_out, grad_mod, keep, send,
    mod, acc_up, acc_down, acc_proj, acc_bias,
):
    step = pl.program_id(0)

    @pl.when(step == 0)
    def _():
        assemble(info, (p0, p1, p2, p3, p4, p5, p6, p7), weights)
        cond_low = silu(conditions[...].astype(F32)).astype(BF)
        mod[...] = dot(cond_low, weights[:, AT_MOD : AT_MOD + MOD_TWO]) + bias_row(
            bias_in[...], ROW_MOD + 6, 12
        )
        acc_up[...] = jnp.zeros_like(acc_up)
        acc_down[...] = jnp.zeros_like(acc_down)
        acc_proj[...] = jnp.zeros_like(acc_proj)
        acc_bias[...] = jnp.zeros_like(acc_bias)
        grad_mod[...] = jnp.zeros_like(grad_mod)

    @pl.when(step >= info[0])
    def _():
        out[0] = jnp.zeros((TOK, D), BF)

    @pl.when(step < info[0])
    def _():
        row = mod[pl.ds(step, 1), :]
        gate_one, shift_two = row[:, :D], row[:, D : 2 * D]
        scale_two, gate_two = row[:, 2 * D : 3 * D], row[:, 3 * D :]
        bias = bias_in[...]
        mixed = mixed_in[0]
        w_proj = weights[:, AT_PROJ : AT_PROJ + D]
        branch_one = dot(mixed, w_proj) + bias_row(bias, ROW_PROJ, 3)
        middle = latents[0].astype(F32) + gate_one * branch_one
        normed, inverse = normalize(middle)
        hidden = (normed * (1.0 + scale_two) + shift_two).astype(BF)
        cot = grad_out[0].astype(F32)
        g_two = (cot * gate_two).astype(BF)
        up_bias = bias_row(bias, ROW_UP, 12)
        branch_two = bias_row(bias, ROW_DOWN, 3)
        d_hidden = jnp.zeros((TOK, D), F32)
        root = 0.7978845608028654
        cube = root * 0.044715
        for chunk in range(4):
            at = D * chunk
            w_up = weights[:, at : at + D]
            w_down = jnp.concatenate(
                [
                    weights[48 * s : 48 * s + 48, AT_DOWN + D * q : AT_DOWN + D * q + D]
                    for s in (2 * chunk, 2 * chunk + 1)
                    for q in range(4)
                ],
                axis=0,
            )
            upward = dot(hidden, w_up) + up_bias[:, at : at + D]
            square = upward * upward
            bend = jnp.tanh(upward * (root + cube * square))
            half = 0.5 + 0.5 * bend
            act = upward * half
            slope = half + act * (1.0 - bend) * (root + (3.0 * cube) * square)
            act_low = act.astype(BF)
            branch_two = branch_two + dot(act_low, w_down)
            acc_down[at : at + D, :] += dot_tn(act_low, g_two)
            g_up = (slope * dot_nt(g_two, w_down)).astype(BF)
            acc_up[:, at : at + D] += dot_tn(hidden, g_up)
            acc_bias[0:1, at : at + D] += jnp.sum(g_up.astype(F32), axis=0, keepdims=True)
            d_hidden = d_hidden + dot_nt(g_up, w_up)
        out[0] = (middle + gate_two * branch_two).astype(BF)
        acc_bias[1:2, :D] += jnp.sum(g_two.astype(F32), axis=0, keepdims=True)
        grad_mod[pl.ds(step, 1), 3 * D :] = jnp.sum(cot * branch_two, axis=0, keepdims=True)
        grad_mod[pl.ds(step, 1), D : 2 * D] = jnp.sum(d_hidden, axis=0, keepdims=True)
        grad_mod[pl.ds(step, 1), 2 * D : 3 * D] = jnp.sum(
            d_hidden * normed, axis=0, keepdims=True
        )
        grad_mid = cot + norm_back(d_hidden * (1.0 + scale_two), normed, inverse)
        grad_mid_out[0] = grad_mid
        grad_mod[pl.ds(step, 1), :D] = jnp.sum(grad_mid * branch_one, axis=0, keepdims=True)
        g_one = (grad_mid * gate_one).astype(BF)
        acc_bias[2:3, :D] += jnp.sum(g_one.astype(F32), axis=0, keepdims=True)
        acc_proj[...] += dot_tn(mixed, g_one)
        grad_mixed_out[0] = dot_nt(g_one, w_proj).astype(BF)

    @pl.when(step == CAP - 1)
    def _():
        cond_low = silu(conditions[...].astype(F32)).astype(BF)
        g_mod = grad_mod[...].astype(BF)
        mod_grad = dot_tn(cond_low.astype(F32), g_mod.astype(F32)).astype(BF)
        z_high, core, column = info[2], info[3], info[1]
        sums = jnp.sum(g_mod.astype(F32), axis=0, keepdims=True)
        rows = [jnp.zeros((ROW_MOD + 6, 128), F32)]
        rows += [sums[:, 128 * i : 128 * i + 128] for i in range(12)]
        rows += [acc_bias[2:3, 128 * i : 128 * i + 128] for i in range(3)]
        rows += [acc_bias[0:1, 128 * i : 128 * i + 128] for i in range(12)]
        rows += [acc_bias[1:2, 128 * i : 128 * i + 128] for i in range(3)]
        rows += [jnp.zeros((3, 128), F32)]
        bias_block = jnp.concatenate(rows, axis=0).astype(BF)
        for owner in range(8):
            zh, xx = owner // 4, owner % 4
            spot = lax.rem(xx - column + 4, 4) * 48
            spot = pl.multiple_of(spot, 16)
            is_mine = (z_high ^ core) == zh
            lo = 48 * owner

            def put(ref, spot=spot, lo=lo, owner=owner):
                ref[pl.ds(spot, 48), :FF] = acc_up[lo : lo + 48, :].astype(BF)
                ref[pl.ds(spot, 48), AT_MOD : AT_MOD + MOD_TWO] = mod_grad[lo : lo + 48, :]
                ref[pl.ds(spot, 48), AT_PROJ : AT_PROJ + D] = acc_proj[lo : lo + 48, :].astype(BF)
                for q in range(4):
                    at = 192 * owner + 48 * q
                    ref[pl.ds(spot, 48), AT_DOWN + D * q : AT_DOWN + D * q + D] = acc_down[
                        at : at + 48, :
                    ].astype(BF)
                ref[pl.ds(spot, 48), BIAS_TWO : BIAS_TWO + 128] = bias_block

            pl.when(is_mine)(functools.partial(put, keep))
            pl.when(jnp.logical_not(is_mine))(functools.partial(put, send))


def backward_kernel(
    info, latents, conditions, qkv_in, expo_in, mixed_in, rinv_in, hidden_in, grad_mid_in,
    grad_mixed_in, mod_in, weights, weights_two, grad_mod_two,
    out, grad_cond, keep, send,
    acc_qkv, acc_bias, grad_mod,
):
    step = pl.program_id(0)

    @pl.when(step == 0)
    def _():
        acc_qkv[...] = jnp.zeros_like(acc_qkv)
        acc_bias[...] = jnp.zeros_like(acc_bias)
        grad_mod[...] = jnp.zeros_like(grad_mod)

    @pl.when(step >= info[0])
    def _():
        out[0] = jnp.zeros((TOK, D), BF)

    @pl.when(step < info[0])
    def _():
        row = mod_in[pl.ds(step, 1), :]
        normed, inverse = normalize(latents[0].astype(F32))
        qkv = qkv_in[0]
        hidden = hidden_in[0]
        scaled = (grad_mixed_in[0].astype(F32) * rinv_in[0]).astype(BF)
        product = scaled.astype(F32) * mixed_in[0].astype(F32)
        low = lax.broadcasted_iota(jnp.int32, (TOK, 128), 1) < HEAD_DIM
        low_wide = lax.broadcasted_iota(jnp.int32, (TOK, 128), 1) < HEAD_DIM
        factor = HEAD_DIM**-0.5
        g_query, g_key, g_value = [], [], []
        for pair in range(HEADS // 2):
            at = 128 * pair
            query = qkv[:, at : at + 128]
            key = qkv[:, D + at : D + at + 128]
            value = qkv[:, 2 * D + at : 2 * D + at + 128]
            grad = scaled[:, at : at + 128]
            weighed = product[:, at : at + 128]
            parts = []
            for half in range(2):
                mask = low if half == 0 else ~low
                chosen = jnp.where(mask, grad, jnp.zeros_like(grad))
                delta = jnp.sum(
                    jnp.where(low_wide if half == 0 else ~low_wide, weighed, 0.0),
                    axis=-1,
                    keepdims=True,
                )
                expo = expo_in[0, 2 * pair + half]
                g_probs = dot_nt(chosen, value)
                g_scores = (expo.astype(F32) * (g_probs - delta)).astype(BF)
                parts.append(
                    (dot(g_scores, key), dot_tn(g_scores, query), dot_tn(expo, grad))
                )
            g_query.append((jnp.where(low_wide, parts[0][0], parts[1][0]) * factor).astype(BF))
            g_key.append((jnp.where(low_wide, parts[0][1], parts[1][1]) * factor).astype(BF))
            g_value.append(jnp.where(low_wide, parts[0][2], parts[1][2]).astype(BF))
        g_qkv = jnp.concatenate(g_query + g_key + g_value, axis=1)
        acc_qkv[...] += dot_tn(hidden, g_qkv)
        acc_bias[0:1, :] += jnp.sum(g_qkv.astype(F32), axis=0, keepdims=True)
        d_hidden = dot_nt(g_qkv, weights[:, :QKV_W])
        grad_mod[pl.ds(step, 1), :D] = jnp.sum(d_hidden, axis=0, keepdims=True)
        grad_mod[pl.ds(step, 1), D:] = jnp.sum(d_hidden * normed, axis=0, keepdims=True)
        out[0] = (
            grad_mid_in[0] + norm_back(d_hidden * (1.0 + row[:, D : 2 * D]), normed, inverse)
        ).astype(BF)

    @pl.when(step == CAP - 1)
    def _():
        cond = conditions[...].astype(F32)
        sig = 1.0 / (1.0 + jnp.exp(-cond))
        cond_low = (cond * sig).astype(BF)
        g_mod = grad_mod[...].astype(BF)
        g_mod_two = grad_mod_two[...].astype(BF)
        g_cond = dot_nt(g_mod, weights[:, QKV_W : QKV_W + MOD_ONE])
        g_cond += dot_nt(g_mod_two, weights_two[:, AT_MOD : AT_MOD + MOD_TWO])
        grad_cond[...] = (g_cond * (sig * (1.0 + cond * (1.0 - sig)))).astype(BF)
        mod_grad = dot_tn(cond_low.astype(F32), g_mod.astype(F32)).astype(BF)
        sums = jnp.sum(g_mod.astype(F32), axis=0, keepdims=True)
        rows = [acc_bias[0:1, 128 * i : 128 * i + 128] for i in range(9)]
        rows += [sums[:, 128 * i : 128 * i + 128] for i in range(6)]
        rows += [jnp.zeros((33, 128), F32)]
        bias_block = jnp.concatenate(rows, axis=0).astype(BF)
        z_high, core, column = info[2], info[3], info[1]
        for owner in range(8):
            zh, xx = owner // 4, owner % 4
            spot = pl.multiple_of(lax.rem(xx - column + 4, 4) * 48, 16)
            is_mine = (z_high ^ core) == zh
            lo = 48 * owner

            def put(ref, spot=spot, lo=lo):
                ref[pl.ds(spot, 48), :QKV_W] = acc_qkv[lo : lo + 48, :].astype(BF)
                ref[pl.ds(spot, 48), QKV_W : QKV_W + MOD_ONE] = mod_grad[lo : lo + 48, :]
                ref[pl.ds(spot, 48), BIAS_ONE : BIAS_ONE + 128] = bias_block

            pl.when(is_mine)(functools.partial(put, keep))
            pl.when(jnp.logical_not(is_mine))(functools.partial(put, send))


def slot_spec(*shape):
    zeros = (0,) * len(shape)
    return pl.BlockSpec((1, *shape), lambda j, info: (jnp.minimum(j, jnp.maximum(info[0] - 1, 0)), *zeros))


def slot_out(*shape):
    zeros = (0,) * len(shape)
    return pl.BlockSpec((1, *shape), lambda j, info: (j, *zeros))


def whole(*shape):
    zeros = (0,) * len(shape)
    return pl.BlockSpec(shape, lambda j, info: zeros)


def params():
    return pltpu.CompilerParams(
        dimension_semantics=("arbitrary",), vmem_limit_bytes=VMEM_BYTES
    )


def run_forward(info, latents, conditions, pieces):
    return pl.pallas_call(
        forward_kernel,
        grid_spec=pltpu.PrefetchScalarGridSpec(
            num_scalar_prefetch=1,
            grid=(CAP,),
            in_specs=[slot_spec(TOK, D), whole(CAP, D)] + [whole(48, LANES_ONE)] * 8,
            out_specs=[
                whole(D, LANES_ONE),
                whole(48, 128),
                whole(CAP, MOD_ONE),
                slot_out(TOK, QKV_W),
                slot_out(HEADS, TOK, TOK),
                slot_out(TOK, D),
                slot_out(TOK, D),
                slot_out(TOK, D),
            ],
        ),
        out_shape=[
            jax.ShapeDtypeStruct((D, LANES_ONE), BF),
            jax.ShapeDtypeStruct((48, 128), F32),
            jax.ShapeDtypeStruct((CAP, MOD_ONE), F32),
            jax.ShapeDtypeStruct((CAP, TOK, QKV_W), BF),
            jax.ShapeDtypeStruct((CAP, HEADS, TOK, TOK), BF),
            jax.ShapeDtypeStruct((CAP, TOK, D), BF),
            jax.ShapeDtypeStruct((CAP, TOK, D), F32),
            jax.ShapeDtypeStruct((CAP, TOK, D), BF),
        ],
        compiler_params=params(),
        name="attention_forward",
        cost_estimate=pl.CostEstimate(
            flops=3_000_000_000, bytes_accessed=20_000_000, transcendentals=3_000_000
        ),
    )(info, latents, conditions, *pieces)


def run_middle(info, latents, conditions, mixed, grad_out, bias, pieces):
    return pl.pallas_call(
        middle_kernel,
        grid_spec=pltpu.PrefetchScalarGridSpec(
            num_scalar_prefetch=1,
            grid=(CAP,),
            in_specs=[
                slot_spec(TOK, D),
                whole(CAP, D),
                slot_spec(TOK, D),
                slot_spec(TOK, D),
                whole(48, 128),
            ]
            + [whole(48, LANES_TWO)] * 8,
            out_specs=[
                whole(D, LANES_TWO),
                slot_out(TOK, D),
                slot_out(TOK, D),
                slot_out(TOK, D),
                whole(CAP, MOD_TWO),
                whole(192, LANES_TWO),
                whole(192, LANES_TWO),
            ],
            scratch_shapes=[
                pltpu.VMEM((CAP, MOD_TWO), F32),
                pltpu.VMEM((D, FF), F32),
                pltpu.VMEM((FF, D), F32),
                pltpu.VMEM((D, D), F32),
                pltpu.VMEM((8, FF), F32),
            ],
        ),
        out_shape=[
            jax.ShapeDtypeStruct((D, LANES_TWO), BF),
            jax.ShapeDtypeStruct((CAP, TOK, D), BF),
            jax.ShapeDtypeStruct((CAP, TOK, D), F32),
            jax.ShapeDtypeStruct((CAP, TOK, D), BF),
            jax.ShapeDtypeStruct((CAP, MOD_TWO), F32),
            jax.ShapeDtypeStruct((192, LANES_TWO), BF),
            jax.ShapeDtypeStruct((192, LANES_TWO), BF),
        ],
        compiler_params=params(),
        name="feed_forward_both_ways",
        cost_estimate=pl.CostEstimate(
            flops=16_000_000_000, bytes_accessed=30_000_000, transcendentals=3_000_000
        ),
    )(info, latents, conditions, mixed, grad_out, bias, *pieces)


def run_backward(
    info, latents, conditions, qkv, expo, mixed, rinv, hidden, grad_mid, grad_mixed, mod,
    weights, weights_two, grad_mod_two,
):
    return pl.pallas_call(
        backward_kernel,
        grid_spec=pltpu.PrefetchScalarGridSpec(
            num_scalar_prefetch=1,
            grid=(CAP,),
            in_specs=[
                slot_spec(TOK, D),
                whole(CAP, D),
                slot_spec(TOK, QKV_W),
                slot_spec(HEADS, TOK, TOK),
                slot_spec(TOK, D),
                slot_spec(TOK, D),
                slot_spec(TOK, D),
                slot_spec(TOK, D),
                slot_spec(TOK, D),
                whole(CAP, MOD_ONE),
                whole(D, LANES_ONE),
                whole(D, LANES_TWO),
                whole(CAP, MOD_TWO),
            ],
            out_specs=[
                slot_out(TOK, D),
                whole(CAP, D),
                whole(192, LANES_ONE),
                whole(192, LANES_ONE),
            ],
            scratch_shapes=[
                pltpu.VMEM((D, QKV_W), F32),
                pltpu.VMEM((8, QKV_W), F32),
                pltpu.VMEM((CAP, MOD_ONE), F32),
            ],
        ),
        out_shape=[
            jax.ShapeDtypeStruct((CAP, TOK, D), BF),
            jax.ShapeDtypeStruct((CAP, D), BF),
            jax.ShapeDtypeStruct((192, LANES_ONE), BF),
            jax.ShapeDtypeStruct((192, LANES_ONE), BF),
        ],
        compiler_params=params(),
        name="attention_backward",
        cost_estimate=pl.CostEstimate(
            flops=9_000_000_000, bytes_accessed=30_000_000, transcendentals=1_000
        ),
    )(
        info, latents, conditions, qkv, expo, mixed, rinv, hidden, grad_mid, grad_mixed, mod,
        weights, weights_two, grad_mod_two,
    )


def place(index):
    shard, rep = divmod(index, 16)
    return shard // 4, shard % 4, rep // 4, (rep // 2) % 2, rep % 2


def index_of(z_high, x, y, z_low, core):
    return (z_high * 4 + x) * 16 + y * 4 + z_low * 2 + core


def routes(target_of):
    return [(i, target_of(*place(i))) for i in range(TWIN)]


def fetch(k):
    def source(zh, x, y, zl, c):
        if c == 0:
            return index_of(zh, (x + k) % 4, y, zl, c)
        return index_of(1 - zh, (x + k) % 4, y, 1 - zl, c)

    return [(source(*place(i)), i) for i in range(TWIN)]


CORE_SWAP = routes(lambda zh, x, y, zl, c: index_of(zh, x, y, zl, 1 - c))
ZLOW_SWAP = routes(lambda zh, x, y, zl, c: index_of(zh, x, y, 1 - zl, c))
BOTH = ("shard", "rep")


def move(value, pairs):
    return lax.ppermute(value, BOTH, pairs)


def y_route(k):
    return routes(lambda zh, x, y, zl, c: index_of(zh, x, (y + k) % 4, zl, c))


def gather(block):
    mine = [move(block, fetch(k)) for k in range(4)]
    other = [move(piece, CORE_SWAP) for piece in mine]
    return mine + other


def add(values, dtype=BF):
    return sum(v.astype(F32) for v in values).astype(dtype)


def reduce(keep, send):
    held = add([keep, move(send, CORE_SWAP)])
    arrived = []
    for k in range(4):
        back = [(target, source) for source, target in fetch(k)]
        arrived.append(move(held[48 * k : 48 * k + 48], back))
    total = add(arrived)
    total = add([total, move(total, CORE_SWAP)])
    total = add([total, move(total, ZLOW_SWAP)])
    return add([total] + [move(total, y_route(k)) for k in (1, 2, 3)], F32)


def pack_bias(shard, mod_bias, qv_bias, proj_bias, up_bias, down_bias):
    flat = jnp.zeros((48 * 128,), BF)
    qv_at = shard * 96 + jnp.where(shard >= 4, D, 0)
    flat = lax.dynamic_update_slice(flat, qv_bias, (qv_at,))
    flat = lax.dynamic_update_slice(flat, mod_bias, (ROW_MOD * 128 + shard * 288,))
    flat = lax.dynamic_update_slice(flat, proj_bias, (ROW_PROJ * 128 + shard * 48,))
    flat = lax.dynamic_update_slice(flat, up_bias, (ROW_UP * 128 + shard * 192,))
    flat = lax.dynamic_update_slice(flat, down_bias, (ROW_DOWN * 128 + shard * 48,))
    return flat.reshape(48, 128)


def on_device(
    latents, conditions, counts, mod_weight, mod_bias, qkv_weight, qv_bias, proj_weight,
    proj_bias, up_weight, up_bias, down_weight, down_bias, grad_out,
):
    shard = lax.axis_index("shard")
    rep = lax.axis_index("rep")
    info = jnp.stack([counts[0], shard % 4, shard // 4, rep % 2]).astype(jnp.int32)
    biases = pack_bias(shard, mod_bias, qv_bias, proj_bias, up_bias, down_bias)
    block_one = jnp.concatenate([qkv_weight, mod_weight[:, :MOD_ONE], biases], axis=1)
    block_two = jnp.concatenate(
        [up_weight, mod_weight[:, MOD_ONE:], proj_weight]
        + [down_weight[48 * q : 48 * q + 48] for q in range(4)]
        + [jnp.zeros((48, 128), BF)],
        axis=1,
    )
    pieces_one = gather(block_one)
    pieces_two = gather(block_two)
    weights, bias, mod, qkv, expo, mixed, rinv, hidden = run_forward(
        info, latents, conditions, pieces_one
    )
    weights_two, out, grad_mid, grad_mixed, grad_mod_two, keep_two, send_two = run_middle(
        info, latents, conditions, mixed, grad_out, bias, pieces_two
    )
    grad_latents, grad_cond, keep_one, send_one = run_backward(
        info, latents, conditions, qkv, expo, mixed, rinv, hidden, grad_mid, grad_mixed, mod,
        weights, weights_two, grad_mod_two,
    )
    two = reduce(keep_two, send_two)
    one = reduce(keep_one, send_one)
    grad_bias = (
        one[:, BIAS_ONE : BIAS_ONE + 128] + two[:, BIAS_TWO : BIAS_TWO + 128]
    ).reshape(-1)
    qv_at = shard * 96 + jnp.where(shard >= 4, D, 0)

    def part(first, size):
        return lax.dynamic_slice(grad_bias, (first,), (size,))

    return (
        out,
        grad_latents,
        grad_cond,
        jnp.concatenate([one[:, QKV_W : QKV_W + MOD_ONE], two[:, AT_MOD : AT_MOD + MOD_TWO]], 1),
        part(ROW_MOD * 128 + shard * 288, 288),
        one[:, :QKV_W],
        part(qv_at, 96),
        two[:, AT_PROJ : AT_PROJ + D],
        part(ROW_PROJ * 128 + shard * 48, 48),
        two[:, :FF],
        part(ROW_UP * 128 + shard * 192, 192),
        jnp.concatenate([two[:, AT_DOWN + D * q : AT_DOWN + D * q + D] for q in range(4)], 0),
        part(ROW_DOWN * 128 + shard * 48, 48),
    )


def solution(mesh):
    slots = P(("shard", "rep"), None, None)
    rows = P(("shard", "rep"), None)
    matrix, vector = P("shard", None), P("shard")
    in_specs = (slots, rows, P(("shard", "rep"))) + (matrix, vector) * 5 + (slots,)
    out_specs = (slots, slots, rows) + (matrix, vector) * 5
    return jax.shard_map(
        on_device, mesh=mesh, in_specs=in_specs, out_specs=out_specs, check_vma=False
    )
```

time: 770 us -> 248 us (0.32)
  waiting for transfers between devices: 383 us -> 74.6 us
  blocking collectives: 182 us -> 0 us
  matrix products: 100 us -> 0 us
  starting transfers between devices: 0.61 us -> 77.1 us
  Pallas kernels: 0 us -> 70.6 us
  other arithmetic: 42.1 us -> 6.25 us
  local copies, waits for them, and re-layouts: 37 us -> 17.5 us
  between operations: 20.8 us -> 1.72 us
    reduce_scatter x5 -> x0, waiting for transfers between devices: 314 us -> none  [the longest x1 78.8 us: on_device(): lax.psum_scatter(grad_mod_full.astype(jnp.bfloat16), 'shard', scatter_dim...]
    dot_general x21 -> x0, matrix products: 100 us -> none  [the longest x5 29 us: back_product(): lax.dot_general(left, right, (((1,), (1,)), ((), ())), preferred_element_...]
    ppermute x0 -> x36, starting transfers between devices: none -> 77.1 us  [move(): return lax.ppermute(value, BOTH, pairs)]
    ppermute x0 -> x36, waiting for transfers between devices: none -> 74.6 us  [move(): return lax.ppermute(value, BOTH, pairs)]
    pallas_call x0 -> x3, Pallas kernels: none -> 70.6 us  [the longest x1 35.4 us: run_middle(): pl.pallas_call(middle_kernel, grid_spec=pltpu.PrefetchScalarGridSpec(num_...]
    unnamed x2 -> x0, blocking collectives: 68.1 us -> none
    psum x1 -> x0, waiting for transfers between devices: 66.9 us -> none  [on_device(): lax.psum(owned[0].astype(jnp.bfloat16), 'rep').astype(jnp.float32)]
    all_gather x2 -> x0, blocking collectives: 61.6 us -> none  [the longest x1 33.3 us: on_device(): lax.all_gather(qkv_weight, 'shard', axis=0, tiled=True)]
  transfers between devices with their start and end apart: 9 -> 36, of which waited for: 6 -> 16; matrix products, arithmetic and copies ran while one was open for 12% -> 4% of each run, Pallas kernels for 0% -> 14%
where the time goes in v1:
time: 248 us
  starting transfers between devices  77.1 us (31%)
  waiting for transfers between devices  74.6 us (30%)
  Pallas kernels  70.6 us (28%)
  local copies, waits for them, and re-layouts  17.5 us (7%)
  other arithmetic  6.25 us (3%)
    ppermute x36, starting transfers between devices, move(): return lax.ppermute(value, BOTH, pairs)  77.1 us
    ppermute x36, waiting for transfers between devices, move(): return lax.ppermute(value, BOTH, pairs)  74.6 us
    pallas_call x1, Pallas kernels, run_middle(): pl.pallas_call(middle_kernel, grid_spec=pltpu.PrefetchScalarGridSpec(num_...  35.4 us
    pallas_call x1, Pallas kernels, run_backward(): pl.pallas_call(backward_kernel, grid_spec=pltpu.PrefetchScalarGridSpec(nu...  21.8 us
    pallas_call x1, Pallas kernels, run_forward(): pl.pallas_call(forward_kernel, grid_spec=pltpu.PrefetchScalarGridSpec(num...  13.4 us
    unnamed x35, local copies, waits for them, and re-layouts  7.62 us
  transfers between devices with their start and end apart: 36, of which 16 were waited for; matrix products, arithmetic and copies ran while one was open for 4% of the time, Pallas kernels for 14%

profile of v1, /device:TPU:1, one launch (start us, length us, event | category | flops | bytes accessed | tf_op | source)
XLA Modules:
  0.0 247.8 jit_solution(9902890866362637753)
XLA Ops:
  6.7 5.6 %collective-permute-start.3 = (bf16[48,2048]{1,0:T(8,128)(2,1)S(1)}, bf16[48,2048]{1,0:T(8,128)(2,1)S(1)}, u32[]{:S(2)}, u32[]{:S(2)}) collective-permute-start(bf16[48,2048]{1,0:T(8,128)(2,1)S(1)} %pad_maximum_fusion.2), channel_id=1, source_target_pairs={{48,0},{115,1},{50,2},{113,3},{52,4},{119,5},{54,6},{117,7},{56,8}... | collective-permute-start | bytes 589832 | tf_op jit(solution)/shard_map/ppermute | solution.py:529
  13.9 4.1 %collective-permute-start.1 = (bf16[48,2048]{1,0:T(8,128)(2,1)S(1)}, bf16[48,2048]{1,0:T(8,128)(2,1)S(1)}, u32[]{:S(2)}, u32[]{:S(2)}) collective-permute-start(bf16[48,2048]{1,0:T(8,128)(2,1)S(1)} %pad_maximum_fusion.2), channel_id=1, source_target_pairs={{16,0},{83,1},{18,2},{81,3},{20,4},{87,5},{22,6},{85,7},{24,8},{91... | collective-permute-start | bytes 589832 | tf_op jit(solution)/shard_map/ppermute | solution.py:529
  25.8 2.8 %collective-permute-start.11 = (bf16[48,5120]{1,0:T(8,128)(2,1)S(1)}, bf16[48,5120]{1,0:T(8,128)(2,1)S(1)}, u32[]{:S(2)}, u32[]{:S(2)}) collective-permute-start(bf16[48,5120]{1,0:T(8,128)(2,1)S(1)} %constant_dynamic-update-slice_fusion), channel_id=1, source_target_pairs={{48,0},{115,1},{50,2},{113,3},{52,4},{119,5},{54,6},{117,7},{56,8}... | collective-permute-start | bytes 1474568 | tf_op jit(solution)/shard_map/ppermute | solution.py:529
  29.4 3.2 %collective-permute-start.9 = (bf16[48,5120]{1,0:T(8,128)(2,1)S(1)}, bf16[48,5120]{1,0:T(8,128)(2,1)S(1)}, u32[]{:S(2)}, u32[]{:S(2)}) collective-permute-start(bf16[48,5120]{1,0:T(8,128)(2,1)S(1)} %constant_dynamic-update-slice_fusion), channel_id=1, source_target_pairs={{16,0},{83,1},{18,2},{81,3},{20,4},{87,5},{22,6},{85,7},{24,8},{91... | collective-permute-start | bytes 1474568 | tf_op jit(solution)/shard_map/ppermute | solution.py:529
  37.0 4.4 %collective-permute-done.11.p3 = bf16[48,5120]{1,0:T(8,128)(2,1)S(1)} collective-permute-done((bf16[48,5120]{1,0:T(8,128)(2,1)S(1)}, bf16[48,5120]{1,0:T(8,128)(2,1)S(1)}, u32[]{:S(2)}, u32[]{:S(2)}) %collective-permute-start.11) | collective-permute-done | bytes 491552 | tf_op jit(solution)/shard_map/ppermute | solution.py:529
  41.4 9.7 %collective-permute-done.10.p2 = bf16[48,5120]{1,0:T(8,128)(2,1)S(1)} collective-permute-done((bf16[48,5120]{1,0:T(8,128)(2,1)S(1)}, bf16[48,5120]{1,0:T(8,128)(2,1)S(1)}, u32[]{:S(2)}, u32[]{:S(2)}) %collective-permute-start.10) | collective-permute-done | bytes 491552 | tf_op jit(solution)/shard_map/ppermute | solution.py:529
  51.1 3.7 %collective-permute-done.9.p1 = bf16[48,5120]{1,0:T(8,128)(2,1)S(1)} collective-permute-done((bf16[48,5120]{1,0:T(8,128)(2,1)S(1)}, bf16[48,5120]{1,0:T(8,128)(2,1)S(1)}, u32[]{:S(2)}, u32[]{:S(2)}) %collective-permute-start.9) | collective-permute-done | bytes 491552 | tf_op jit(solution)/shard_map/ppermute | solution.py:529
  58.0 13.4 %attention_forward.1 = (bf16[384,2048]{1,0:T(8,128)(2,1)}, f32[48,128]{1,0:T(8,128)}, f32[8,768]{1,0:T(8,128)}, bf16[8,256,1152]{2,1,0:T(8,128)(2,1)}, bf16[8,6,...) custom-call(s32[4]{0:T(128)} %pad_add_fusion.info, ...), custom_call_target="tpu_custom_call" | custom-call | flops 3000000000 | bytes 20000000 | tf_op jit(solution)/shard_map/attention_forward/pallas_call | solution.py:365
  72.5 35.4 %feed_forward_both_ways.1 = (bf16[384,5120]{1,0:T(8,128)(2,1)}, bf16[8,256,384]{2,1,0:T(8,128)(2,1)}, f32[8,256,384]{2,1,0:T(8,128)}, bf16[8,256,384]{2,1,0:T(8,...) custom-call(s32[4]{0:T(128)} %pad_add_fusion.info, ...), custom_call_target="tpu_custom_call" | custom-call | flops 16000000000 | bytes 30000000 | tf_op jit(solution)/shard_map/feed_forward_both_ways/pallas_call | solution.py:401
  108.0 11.6 %collective-permute-start.26 = (bf16[192,5120]{1,0:T(8,128)(2,1)}, bf16[192,5120]{1,0:T(8,128)(2,1)S(1)}, u32[]{:S(2)}, u32[]{:S(2)}) collective-permute-start(bf16[192,5120]{1,0:T(8,128)(2,1)} %get-tuple-element.50), channel_id=1, source_target_pairs={{0,1},{1,0},{2,3},{3,2},{4,5},{5,4},{6,7},{7,6},{8,9},{9,8},{10,11... | collective-permute-start | bytes 5898248 | tf_op jit(solution)/shard_map/ppermute | solution.py:529
  119.5 21.8 %attention_backward.1 = (bf16[8,256,384]{2,1,0:T(8,128)(2,1)}, bf16[8,384]{1,0:T(8,128)(2,1)}, bf16[192,2048]{1,0:T(8,128)(2,1)}, bf16[192,2048]{1,0:T(8,128)(2,1)}) custom-call(s32[4]{0:T(128)} %pad_add_fusion.info, bf16[8,256,384]{2,1,0:T(8,128)(2,1)} %latents.5, bf16[8,384]{1,0:T(8,128)(2,1)} %conditions.5, ...), custom_call_target="tpu_custom_call" | custom-call | flops 8999999488 | bytes 30000000 | tf_op jit(solution)/shard_map/attention_backward/pallas_call | solution.py:452
  141.3 5.1 %collective-permute-start.16 = (bf16[192,2048]{1,0:T(8,128)(2,1)}, bf16[192,2048]{1,0:T(8,128)(2,1)S(1)}, u32[]{:S(2)}, u32[]{:S(2)}) collective-permute-start(bf16[192,2048]{1,0:T(8,128)(2,1)} %get-tuple-element.48), channel_id=1, source_target_pairs={{0,1},{1,0},{2,3},{3,2},{4,5},{5,4},{6,7},{7,6},{8,9},{9,8},{10,11... | collective-permute-start | bytes 2359304 | tf_op jit(solution)/shard_map/ppermute | solution.py:529
  150.1 4.6 %collective-permute-start.17 = (bf16[48,2048]{1,0:T(8,128)(2,1)S(1)}, bf16[48,2048]{1,0:T(8,128)(2,1)S(1)}, u32[]{:S(2)}, u32[]{:S(2)}) collective-permute-start(bf16[48,2048]{1,0:T(8,128)(2,1)S(1)} %get-tuple-element.62), channel_id=1, source_target_pairs={{0,0},{1,67},{2,2},{3,65},{4,4},{5,71},{6,6},{7,69},{8,8},{9,75},{... | collective-permute-start | bytes 589832 | tf_op jit(solution)/shard_map/ppermute | solution.py:529
  154.8 8.4 %collective-permute-start.19 = (bf16[48,2048]{1,0:T(8,128)(2,1)S(1)}, bf16[48,2048]{1,0:T(8,128)(2,1)S(1)}, u32[]{:S(2)}, u32[]{:S(2)}) collective-permute-start(bf16[48,2048]{1,0:T(8,128)(2,1)S(1)} %get-tuple-element.64), channel_id=1, source_target_pairs={{0,32},{1,99},{2,34},{3,97},{4,36},{5,103},{6,38},{7,101},{8,40},{... | collective-permute-start | bytes 589832 | tf_op jit(solution)/shard_map/ppermute | solution.py:529
  163.2 2.9 %collective-permute-start.18 = (bf16[48,2048]{1,0:T(8,128)(2,1)S(1)}, bf16[48,2048]{1,0:T(8,128)(2,1)S(1)}, u32[]{:S(2)}, u32[]{:S(2)}) collective-permute-start(bf16[48,2048]{1,0:T(8,128)(2,1)S(1)} %get-tuple-element.65), channel_id=1, source_target_pairs={{0,16},{1,83},{2,18},{3,81},{4,20},{5,87},{6,22},{7,85},{8,24},{9,... | collective-permute-start | bytes 589832 | tf_op jit(solution)/shard_map/ppermute | solution.py:529
  166.9 4.6 %collective-permute-start.27 = (bf16[48,5120]{1,0:T(8,128)(2,1)S(1)}, bf16[48,5120]{1,0:T(8,128)(2,1)S(1)}, u32[]{:S(2)}, u32[]{:S(2)}) collective-permute-start(bf16[48,5120]{1,0:T(8,128)(2,1)S(1)} %get-tuple-element.51), channel_id=1, source_target_pairs={{0,0},{1,67},{2,2},{3,65},{4,4},{5,71},{6,6},{7,69},{8,8},{9,75},{... | collective-permute-start | bytes 1474568 | tf_op jit(solution)/shard_map/ppermute | solution.py:529
  175.9 17.7 %collective-permute-done.27 = bf16[48,5120]{1,0:T(8,128)(2,1)S(1)} collective-permute-done((bf16[48,5120]{1,0:T(8,128)(2,1)S(1)}, bf16[48,5120]{1,0:T(8,128)(2,1)S(1)}, u32[]{:S(2)}, u32[]{:S(2)}) %collective-permute-start.27) | collective-permute-done | bytes 491552 | tf_op jit(solution)/shard_map/ppermute | solution.py:529
  196.9 4.1 %collective-permute-done.22 = bf16[48,2048]{1,0:T(8,128)(2,1)S(1)} collective-permute-done((bf16[48,2048]{1,0:T(8,128)(2,1)S(1)}, bf16[48,2048]{1,0:T(8,128)(2,1)S(1)}, u32[]{:S(2)}, u32[]{:S(2)}) %collective-permute-start.22) | collective-permute-done | bytes 196640 | tf_op jit(solution)/shard_map/ppermute | solution.py:529
  201.0 5.3 %collective-permute-start.25 = (bf16[48,2048]{1,0:T(8,128)(2,1)S(1)}, bf16[48,2048]{1,0:T(8,128)(2,1)S(1)}, u32[]{:S(2)}, u32[]{:S(2)}) collective-permute-start(bf16[48,2048]{1,0:T(8,128)(2,1)S(1)} %add_convert_fusion.5), channel_id=1, source_target_pairs={{0,12},{1,13},{2,14},{3,15},{4,0},{5,1},{6,2},{7,3},{8,4},{9,5},{1... | collective-permute-start | bytes 589832 | tf_op jit(solution)/shard_map/ppermute | solution.py:529
  207.0 4.5 %collective-permute-done.32 = bf16[48,5120]{1,0:T(8,128)(2,1)S(1)} collective-permute-done((bf16[48,5120]{1,0:T(8,128)(2,1)S(1)}, bf16[48,5120]{1,0:T(8,128)(2,1)S(1)}, u32[]{:S(2)}, u32[]{:S(2)}) %collective-permute-start.32) | collective-permute-done | bytes 491552 | tf_op jit(solution)/shard_map/ppermute | solution.py:529
  211.6 5.3 %collective-permute-start.35 = (bf16[48,5120]{1,0:T(8,128)(2,1)S(1)}, bf16[48,5120]{1,0:T(8,128)(2,1)S(1)}, u32[]{:S(2)}, u32[]{:S(2)}) collective-permute-start(bf16[48,5120]{1,0:T(8,128)(2,1)S(1)} %add_convert_fusion.2), channel_id=1, source_target_pairs={{0,12},{1,13},{2,14},{3,15},{4,0},{5,1},{6,2},{7,3},{8,4},{9,5},{1... | collective-permute-start | bytes 1474568 | tf_op jit(solution)/shard_map/ppermute | solution.py:529
  218.6 8.4 %collective-permute-done.35 = bf16[48,5120]{1,0:T(8,128)(2,1)S(1)} collective-permute-done((bf16[48,5120]{1,0:T(8,128)(2,1)S(1)}, bf16[48,5120]{1,0:T(8,128)(2,1)S(1)}, u32[]{:S(2)}, u32[]{:S(2)}) %collective-permute-start.35) | collective-permute-done | bytes 491552 | tf_op jit(solution)/shard_map/ppermute | solution.py:529
  227.0 2.7 %collective-permute-done.34 = bf16[48,5120]{1,0:T(8,128)(2,1)S(1)} collective-permute-done((bf16[48,5120]{1,0:T(8,128)(2,1)S(1)}, bf16[48,5120]{1,0:T(8,128)(2,1)S(1)}, u32[]{:S(2)}, u32[]{:S(2)}) %collective-permute-start.34) | collective-permute-done | bytes 491552 | tf_op jit(solution)/shard_map/ppermute | solution.py:529
  229.6 12.5 %collective-permute-done.33 = bf16[48,5120]{1,0:T(8,128)(2,1)S(1)} collective-permute-done((bf16[48,5120]{1,0:T(8,128)(2,1)S(1)}, bf16[48,5120]{1,0:T(8,128)(2,1)S(1)}, u32[]{:S(2)}, u32[]{:S(2)}) %collective-permute-start.33) | collective-permute-done | bytes 491552 | tf_op jit(solution)/shard_map/ppermute | solution.py:529
  (119 shorter events, 44.6 us)
Async XLA Ops:
  6.7 19.0 %collective-permute-start.3 = (bf16[48,2048]{1,0:T(8,128)(2,1)S(1)}, bf16[48,2048]{1,0:T(8,128)(2,1)S(1)}, u32[]{:S(2)}, u32[]{:S(2)}) collective-permute-start(bf16[48,2048]{1,0:T(8,128)(2,1)S(1)} %pad_maximum_fusion.2), channel_id=1, source_target_pairs={{48,0},{115,1},{50,2},{113,3},{52,4},{119,5},{54,6},{117,7},{56,8}... | collective-permute-start | bytes 589832 | tf_op jit(solution)/shard_map/ppermute | solution.py:529
  12.3 16.3 %collective-permute-start.2 = (bf16[48,2048]{1,0:T(8,128)(2,1)S(1)}, bf16[48,2048]{1,0:T(8,128)(2,1)S(1)}, u32[]{:S(2)}, u32[]{:S(2)}) collective-permute-start(bf16[48,2048]{1,0:T(8,128)(2,1)S(1)} %pad_maximum_fusion.2), channel_id=1, source_target_pairs={{32,0},{99,1},{34,2},{97,3},{36,4},{103,5},{38,6},{101,7},{40,8},{... | collective-permute-start | bytes 589832 | tf_op jit(solution)/shard_map/ppermute | solution.py:529
  13.9 15.5 %collective-permute-start.1 = (bf16[48,2048]{1,0:T(8,128)(2,1)S(1)}, bf16[48,2048]{1,0:T(8,128)(2,1)S(1)}, u32[]{:S(2)}, u32[]{:S(2)}) collective-permute-start(bf16[48,2048]{1,0:T(8,128)(2,1)S(1)} %pad_maximum_fusion.2), channel_id=1, source_target_pairs={{16,0},{83,1},{18,2},{81,3},{20,4},{87,5},{22,6},{85,7},{24,8},{91... | collective-permute-start | bytes 589832 | tf_op jit(solution)/shard_map/ppermute | solution.py:529
  25.8 15.6 %collective-permute-start.11 = (bf16[48,5120]{1,0:T(8,128)(2,1)S(1)}, bf16[48,5120]{1,0:T(8,128)(2,1)S(1)}, u32[]{:S(2)}, u32[]{:S(2)}) collective-permute-start(bf16[48,5120]{1,0:T(8,128)(2,1)S(1)} %constant_dynamic-update-slice_fusion), channel_id=1, source_target_pairs={{48,0},{115,1},{50,2},{113,3},{52,4},{119,5},{54,6},{117,7},{56,8}... | collective-permute-start | bytes 1474568 | tf_op jit(solution)/shard_map/ppermute | solution.py:529
  28.5 22.6 %collective-permute-start.10 = (bf16[48,5120]{1,0:T(8,128)(2,1)S(1)}, bf16[48,5120]{1,0:T(8,128)(2,1)S(1)}, u32[]{:S(2)}, u32[]{:S(2)}) collective-permute-start(bf16[48,5120]{1,0:T(8,128)(2,1)S(1)} %constant_dynamic-update-slice_fusion), channel_id=1, source_target_pairs={{32,0},{99,1},{34,2},{97,3},{36,4},{103,5},{38,6},{101,7},{40,8},{... | collective-permute-start | bytes 1474568 | tf_op jit(solution)/shard_map/ppermute | solution.py:529
  29.4 25.3 %collective-permute-start.9 = (bf16[48,5120]{1,0:T(8,128)(2,1)S(1)}, bf16[48,5120]{1,0:T(8,128)(2,1)S(1)}, u32[]{:S(2)}, u32[]{:S(2)}) collective-permute-start(bf16[48,5120]{1,0:T(8,128)(2,1)S(1)} %constant_dynamic-update-slice_fusion), channel_id=1, source_target_pairs={{16,0},{83,1},{18,2},{81,3},{20,4},{87,5},{22,6},{85,7},{24,8},{91... | collective-permute-start | bytes 1474568 | tf_op jit(solution)/shard_map/ppermute | solution.py:529
  32.7 22.7 %collective-permute-start.8 = (bf16[48,5120]{1,0:T(8,128)(2,1)S(1)}, bf16[48,5120]{1,0:T(8,128)(2,1)S(1)}, u32[]{:S(2)}, u32[]{:S(2)}) collective-permute-start(bf16[48,5120]{1,0:T(8,128)(2,1)S(1)} %constant_dynamic-update-slice_fusion), channel_id=1, source_target_pairs={{0,0},{67,1},{2,2},{65,3},{4,4},{71,5},{6,6},{69,7},{8,8},{75,9},{... | collective-permute-start | bytes 1474568 | tf_op jit(solution)/shard_map/ppermute | solution.py:529
  36.9 18.5 %collective-permute-start.5 = (bf16[48,2048]{1,0:T(8,128)(2,1)S(1)}, bf16[48,2048]{1,0:T(8,128)(2,1)S(1)}, u32[]{:S(2)}, u32[]{:S(2)}) collective-permute-start(bf16[48,2048]{1,0:T(8,128)(2,1)S(1)} %collective-permute-done.1.p1), channel_id=1, source_target_pairs={{0,1},{1,0},{2,3},{3,2},{4,5},{5,4},{6,7},{7,6},{8,9},{9,8},{10,11... | collective-permute-start | bytes 589832 | tf_op jit(solution)/shard_map/ppermute | solution.py:529
  41.4 30.0 %collective-permute-start.15 = (bf16[48,5120]{1,0:T(8,128)(2,1)S(1)}, bf16[48,5120]{1,0:T(8,128)(2,1)S(1)}, u32[]{:S(2)}, u32[]{:S(2)}) collective-permute-start(bf16[48,5120]{1,0:T(8,128)(2,1)S(1)} %collective-permute-done.11.p3), channel_id=1, source_target_pairs={{0,1},{1,0},{2,3},{3,2},{4,5},{5,4},{6,7},{7,6},{8,9},{9,8},{10,11... | collective-permute-start | bytes 1474568 | tf_op jit(solution)/shard_map/ppermute | solution.py:529
  51.1 20.3 %collective-permute-start.14 = (bf16[48,5120]{1,0:T(8,128)(2,1)S(1)}, bf16[48,5120]{1,0:T(8,128)(2,1)S(1)}, u32[]{:S(2)}, u32[]{:S(2)}) collective-permute-start(bf16[48,5120]{1,0:T(8,128)(2,1)S(1)} %collective-permute-done.10.p2), channel_id=1, source_target_pairs={{0,1},{1,0},{2,3},{3,2},{4,5},{5,4},{6,7},{7,6},{8,9},{9,8},{10,11... | collective-permute-start | bytes 1474568 | tf_op jit(solution)/shard_map/ppermute | solution.py:529
  54.8 16.7 %collective-permute-start.13 = (bf16[48,5120]{1,0:T(8,128)(2,1)S(1)}, bf16[48,5120]{1,0:T(8,128)(2,1)S(1)}, u32[]{:S(2)}, u32[]{:S(2)}) collective-permute-start(bf16[48,5120]{1,0:T(8,128)(2,1)S(1)} %collective-permute-done.9.p1), channel_id=1, source_target_pairs={{0,1},{1,0},{2,3},{3,2},{4,5},{5,4},{6,7},{7,6},{8,9},{9,8},{10,11... | collective-permute-start | bytes 1474568 | tf_op jit(solution)/shard_map/ppermute | solution.py:529
  55.4 16.1 %collective-permute-start.12 = (bf16[48,5120]{1,0:T(8,128)(2,1)S(1)}, bf16[48,5120]{1,0:T(8,128)(2,1)}, u32[]{:S(2)}, u32[]{:S(2)}) collective-permute-start(bf16[48,5120]{1,0:T(8,128)(2,1)S(1)} %collective-permute-done.8.p0), channel_id=1, source_target_pairs={{0,1},{1,0},{2,3},{3,2},{4,5},{5,4},{6,7},{7,6},{8,9},{9,8},{10,11... | collective-permute-start | bytes 1474568 | tf_op jit(solution)/shard_map/ppermute | solution.py:529
  108.0 58.1 %collective-permute-start.26 = (bf16[192,5120]{1,0:T(8,128)(2,1)}, bf16[192,5120]{1,0:T(8,128)(2,1)S(1)}, u32[]{:S(2)}, u32[]{:S(2)}) collective-permute-start(bf16[192,5120]{1,0:T(8,128)(2,1)} %get-tuple-element.50), channel_id=1, source_target_pairs={{0,1},{1,0},{2,3},{3,2},{4,5},{5,4},{6,7},{7,6},{8,9},{9,8},{10,11... | collective-permute-start | bytes 5898248 | tf_op jit(solution)/shard_map/ppermute | solution.py:529
  150.1 21.3 %collective-permute-start.17 = (bf16[48,2048]{1,0:T(8,128)(2,1)S(1)}, bf16[48,2048]{1,0:T(8,128)(2,1)S(1)}, u32[]{:S(2)}, u32[]{:S(2)}) collective-permute-start(bf16[48,2048]{1,0:T(8,128)(2,1)S(1)} %get-tuple-element.62), channel_id=1, source_target_pairs={{0,0},{1,67},{2,2},{3,65},{4,4},{5,71},{6,6},{7,69},{8,8},{9,75},{... | collective-permute-start | bytes 589832 | tf_op jit(solution)/shard_map/ppermute | solution.py:529
  154.7 18.7 %collective-permute-start.20 = (bf16[48,2048]{1,0:T(8,128)(2,1)S(1)}, bf16[48,2048]{1,0:T(8,128)(2,1)S(1)}, u32[]{:S(2)}, u32[]{:S(2)}) collective-permute-start(bf16[48,2048]{1,0:T(8,128)(2,1)S(1)} %get-tuple-element.63), channel_id=1, source_target_pairs={{0,48},{1,115},{2,50},{3,113},{4,52},{5,119},{6,54},{7,117},{8,56}... | collective-permute-start | bytes 589832 | tf_op jit(solution)/shard_map/ppermute | solution.py:529
  154.8 18.7 %collective-permute-start.19 = (bf16[48,2048]{1,0:T(8,128)(2,1)S(1)}, bf16[48,2048]{1,0:T(8,128)(2,1)S(1)}, u32[]{:S(2)}, u32[]{:S(2)}) collective-permute-start(bf16[48,2048]{1,0:T(8,128)(2,1)S(1)} %get-tuple-element.64), channel_id=1, source_target_pairs={{0,32},{1,99},{2,34},{3,97},{4,36},{5,103},{6,38},{7,101},{8,40},{... | collective-permute-start | bytes 589832 | tf_op jit(solution)/shard_map/ppermute | solution.py:529
  166.9 26.7 %collective-permute-start.27 = (bf16[48,5120]{1,0:T(8,128)(2,1)S(1)}, bf16[48,5120]{1,0:T(8,128)(2,1)S(1)}, u32[]{:S(2)}, u32[]{:S(2)}) collective-permute-start(bf16[48,5120]{1,0:T(8,128)(2,1)S(1)} %get-tuple-element.51), channel_id=1, source_target_pairs={{0,0},{1,67},{2,2},{3,65},{4,4},{5,71},{6,6},{7,69},{8,8},{9,75},{... | collective-permute-start | bytes 1474568 | tf_op jit(solution)/shard_map/ppermute | solution.py:529
  171.5 22.1 %collective-permute-start.30 = (bf16[48,5120]{1,0:T(8,128)(2,1)S(1)}, bf16[48,5120]{1,0:T(8,128)(2,1)S(1)}, u32[]{:S(2)}, u32[]{:S(2)}) collective-permute-start(bf16[48,5120]{1,0:T(8,128)(2,1)S(1)} %get-tuple-element.52), channel_id=1, source_target_pairs={{0,48},{1,115},{2,50},{3,113},{4,52},{5,119},{6,54},{7,117},{8,56}... | collective-permute-start | bytes 1474568 | tf_op jit(solution)/shard_map/ppermute | solution.py:529
  173.5 20.1 %collective-permute-start.29 = (bf16[48,5120]{1,0:T(8,128)(2,1)S(1)}, bf16[48,5120]{1,0:T(8,128)(2,1)S(1)}, u32[]{:S(2)}, u32[]{:S(2)}) collective-permute-start(bf16[48,5120]{1,0:T(8,128)(2,1)S(1)} %get-tuple-element.53), channel_id=1, source_target_pairs={{0,32},{1,99},{2,34},{3,97},{4,36},{5,103},{6,38},{7,101},{8,40},{... | collective-permute-start | bytes 1474568 | tf_op jit(solution)/shard_map/ppermute | solution.py:529
  173.5 21.1 %collective-permute-start.28 = (bf16[48,5120]{1,0:T(8,128)(2,1)S(1)}, bf16[48,5120]{1,0:T(8,128)(2,1)S(1)}, u32[]{:S(2)}, u32[]{:S(2)}) collective-permute-start(bf16[48,5120]{1,0:T(8,128)(2,1)S(1)} %get-tuple-element.54), channel_id=1, source_target_pairs={{0,16},{1,83},{2,18},{3,81},{4,20},{5,87},{6,22},{7,85},{8,24},{9,... | collective-permute-start | bytes 1474568 | tf_op jit(solution)/shard_map/ppermute | solution.py:529
  175.8 19.1 %collective-permute-start.21 = (bf16[48,2048]{1,0:T(8,128)(2,1)S(1)}, bf16[48,2048]{1,0:T(8,128)(2,1)S(1)}, u32[]{:S(2)}, u32[]{:S(2)}) collective-permute-start(bf16[48,2048]{1,0:T(8,128)(2,1)S(1)} %add_convert_fusion.7), channel_id=1, source_target_pairs={{0,1},{1,0},{2,3},{3,2},{4,5},{5,4},{6,7},{7,6},{8,9},{9,8},{10,11... | collective-permute-start | bytes 589832 | tf_op jit(solution)/shard_map/ppermute | solution.py:529
  201.0 16.4 %collective-permute-start.25 = (bf16[48,2048]{1,0:T(8,128)(2,1)S(1)}, bf16[48,2048]{1,0:T(8,128)(2,1)S(1)}, u32[]{:S(2)}, u32[]{:S(2)}) collective-permute-start(bf16[48,2048]{1,0:T(8,128)(2,1)S(1)} %add_convert_fusion.5), channel_id=1, source_target_pairs={{0,12},{1,13},{2,14},{3,15},{4,0},{5,1},{6,2},{7,3},{8,4},{9,5},{1... | collective-permute-start | bytes 589832 | tf_op jit(solution)/shard_map/ppermute | solution.py:529
  211.6 15.3 %collective-permute-start.35 = (bf16[48,5120]{1,0:T(8,128)(2,1)S(1)}, bf16[48,5120]{1,0:T(8,128)(2,1)S(1)}, u32[]{:S(2)}, u32[]{:S(2)}) collective-permute-start(bf16[48,5120]{1,0:T(8,128)(2,1)S(1)} %add_convert_fusion.2), channel_id=1, source_target_pairs={{0,12},{1,13},{2,14},{3,15},{4,0},{5,1},{6,2},{7,3},{8,4},{9,5},{1... | collective-permute-start | bytes 1474568 | tf_op jit(solution)/shard_map/ppermute | solution.py:529
  217.4 24.7 %collective-permute-start.33 = (bf16[48,5120]{1,0:T(8,128)(2,1)S(1)}, bf16[48,5120]{1,0:T(8,128)(2,1)S(1)}, u32[]{:S(2)}, u32[]{:S(2)}) collective-permute-start(bf16[48,5120]{1,0:T(8,128)(2,1)S(1)} %add_convert_fusion.2), channel_id=1, source_target_pairs={{0,4},{1,5},{2,6},{3,7},{4,8},{5,9},{6,10},{7,11},{8,12},{9,13},{1... | collective-permute-start | bytes 1474568 | tf_op jit(solution)/shard_map/ppermute | solution.py:529
  (26 other events, 330.0 us)

commit v2 on v1

--- a/solution.py
+++ b/solution.py
@@ -58,6 +58,33 @@
     return inverse * (grad - first - normed * second)
 
 
+def spread(rows, size):
+    width = 8 * size
+    lane = lax.broadcasted_iota(jnp.int32, (8, width), 1)
+    total = jnp.zeros((8, width), F32)
+    for owner, row in enumerate(rows):
+        padded = jnp.concatenate([row, jnp.zeros((1, width - row.shape[1]), F32)], axis=1)
+        padded = jnp.where(lane < size, jnp.broadcast_to(padded, (8, width)), 0.0)
+        total += pltpu.roll(padded, owner * size, 1) if owner else padded
+    return total[0:1]
+
+
+def all_biases(raw):
+    def rows(first, count):
+        return [
+            jnp.concatenate([block[first + i : first + i + 1] for i in range(count)], axis=1)
+            for block in raw
+        ]
+
+    qv = spread(rows(0, 1), 96)
+    full = [qv[:, :D], jnp.zeros((1, D), F32), qv[:, D:]]
+    full += [spread(rows(1, 3), 288), spread(rows(4, 1), 48)]
+    full += [spread(rows(5, 2), 192), spread(rows(7, 1), 48)]
+    full = jnp.concatenate(full, axis=1)
+    cut = [full[:, 128 * i : 128 * i + 128] for i in range(45)]
+    return jnp.concatenate(cut + [jnp.zeros((3, 128), F32)], axis=0)
+
+
 def bias_row(bias, first, count):
     return jnp.concatenate([bias[first + i : first + i + 1, :] for i in range(count)], axis=1)
 
@@ -85,9 +112,12 @@
     @pl.when(step == 0)
     def _():
         assemble(info, (p0, p1, p2, p3, p4, p5, p6, p7), weights)
-        total = jnp.zeros((48, 128), F32)
-        for k in range(8):
-            total += weights[48 * k : 48 * k + 48, BIAS_ONE : BIAS_ONE + 128].astype(F32)
+        total = all_biases(
+            [
+                weights[48 * k : 48 * k + 16, BIAS_ONE : BIAS_ONE + 128].astype(F32)[:8]
+                for k in range(8)
+            ]
+        )
         bias_out[...] = total
         cond_low = silu(conditions[...].astype(F32)).astype(BF)
         mod_out[...] = dot(cond_low, weights[:, QKV_W : QKV_W + MOD_ONE]) + bias_row(
@@ -99,10 +129,10 @@
         mod = mod_out[pl.ds(step, 1), :]
         normed, _ = normalize(latents[0].astype(F32))
         hidden = (normed * (1.0 + mod[:, D : 2 * D]) + mod[:, :D]).astype(BF)
-        hidden_out[0] = hidden
+        hidden_out[step] = hidden
         full_bias = bias_row(bias_out[0:16, :], ROW_QKV, 9)
         qkv = (dot(hidden, weights[:, :QKV_W]) + full_bias).astype(BF)
-        qkv_out[0] = qkv
+        qkv_out[step] = qkv
         low = lax.broadcasted_iota(jnp.int32, (TOK, 128), 1) < HEAD_DIM
         ones = jnp.ones((TOK, 128), BF)
         for pair in range(HEADS // 2):
@@ -115,12 +145,12 @@
                 chosen = jnp.where(low if half == 0 else ~low, query, jnp.zeros_like(query))
                 scores = dot_nt(chosen, key)
                 expo = jnp.exp(scores - jnp.max(scores, axis=-1, keepdims=True)).astype(BF)
-                expo_out[0, 2 * pair + half] = expo
+                expo_out[step, 2 * pair + half] = expo
                 parts.append(dot(expo, value))
             total = jnp.where(low, parts[0][:, 128:], parts[1][:, 128:])
             inverse = 1.0 / total
-            rinv_out[0, :, at : at + 128] = inverse
-            mixed_out[0, :, at : at + 128] = (
+            rinv_out[step, :, at : at + 128] = inverse
+            mixed_out[step, :, at : at + 128] = (
                 jnp.where(low, parts[0][:, :128], parts[1][:, :128]) * inverse
             ).astype(BF)
 
@@ -155,7 +185,7 @@
         gate_one, shift_two = row[:, :D], row[:, D : 2 * D]
         scale_two, gate_two = row[:, 2 * D : 3 * D], row[:, 3 * D :]
         bias = bias_in[...]
-        mixed = mixed_in[0]
+        mixed = mixed_in[step]
         w_proj = weights[:, AT_PROJ : AT_PROJ + D]
         branch_one = dot(mixed, w_proj) + bias_row(bias, ROW_PROJ, 3)
         middle = latents[0].astype(F32) + gate_one * branch_one
@@ -200,12 +230,12 @@
             d_hidden * normed, axis=0, keepdims=True
         )
         grad_mid = cot + norm_back(d_hidden * (1.0 + scale_two), normed, inverse)
-        grad_mid_out[0] = grad_mid
+        grad_mid_out[step] = grad_mid
         grad_mod[pl.ds(step, 1), :D] = jnp.sum(grad_mid * branch_one, axis=0, keepdims=True)
         g_one = (grad_mid * gate_one).astype(BF)
         acc_bias[2:3, :D] += jnp.sum(g_one.astype(F32), axis=0, keepdims=True)
         acc_proj[...] += dot_tn(mixed, g_one)
-        grad_mixed_out[0] = dot_nt(g_one, w_proj).astype(BF)
+        grad_mixed_out[step] = dot_nt(g_one, w_proj).astype(BF)
 
     @pl.when(step == CAP - 1)
     def _():
@@ -244,31 +274,41 @@
 
 
 def backward_kernel(
+    first, last,
     info, latents, conditions, qkv_in, expo_in, mixed_in, rinv_in, hidden_in, grad_mid_in,
-    grad_mixed_in, mod_in, weights, weights_two, grad_mod_two,
-    out, grad_cond, keep, send,
-    acc_qkv, acc_bias, grad_mod,
+    grad_mixed_in, mod_in, weights, *refs,
 ):
+    if last:
+        weights_two, grad_mod_two, acc_in, bias_in, grad_mod_in, _, out, grad_cond, keep, send = refs[:10]
+        acc_qkv, acc_bias, grad_mod = refs[10:]
+    else:
+        out, acc_qkv, acc_bias, grad_mod = refs
     step = pl.program_id(0)
+    slot = step + first
 
     @pl.when(step == 0)
     def _():
-        acc_qkv[...] = jnp.zeros_like(acc_qkv)
-        acc_bias[...] = jnp.zeros_like(acc_bias)
-        grad_mod[...] = jnp.zeros_like(grad_mod)
-
-    @pl.when(step >= info[0])
+        if last:
+            acc_qkv[...] = acc_in[...]
+            acc_bias[...] = bias_in[...]
+            grad_mod[...] = grad_mod_in[...]
+        else:
+            acc_qkv[...] = jnp.zeros_like(acc_qkv)
+            acc_bias[...] = jnp.zeros_like(acc_bias)
+            grad_mod[...] = jnp.zeros_like(grad_mod)
+
+    @pl.when(slot >= info[0])
     def _():
         out[0] = jnp.zeros((TOK, D), BF)
 
-    @pl.when(step < info[0])
-    def _():
-        row = mod_in[pl.ds(step, 1), :]
+    @pl.when(slot < info[0])
+    def _():
+        row = mod_in[pl.ds(slot, 1), :]
         normed, inverse = normalize(latents[0].astype(F32))
-        qkv = qkv_in[0]
-        hidden = hidden_in[0]
-        scaled = (grad_mixed_in[0].astype(F32) * rinv_in[0]).astype(BF)
-        product = scaled.astype(F32) * mixed_in[0].astype(F32)
+        qkv = qkv_in[slot]
+        hidden = hidden_in[slot]
+        scaled = (grad_mixed_in[slot].astype(F32) * rinv_in[slot]).astype(BF)
+        product = scaled.astype(F32) * mixed_in[slot].astype(F32)
         low = lax.broadcasted_iota(jnp.int32, (TOK, 128), 1) < HEAD_DIM
         low_wide = lax.broadcasted_iota(jnp.int32, (TOK, 128), 1) < HEAD_DIM
         factor = HEAD_DIM**-0.5
@@ -289,7 +329,7 @@
                     axis=-1,
                     keepdims=True,
                 )
-                expo = expo_in[0, 2 * pair + half]
+                expo = expo_in[slot, 2 * pair + half]
                 g_probs = dot_nt(chosen, value)
                 g_scores = (expo.astype(F32) * (g_probs - delta)).astype(BF)
                 parts.append(
@@ -302,13 +342,16 @@
         acc_qkv[...] += dot_tn(hidden, g_qkv)
         acc_bias[0:1, :] += jnp.sum(g_qkv.astype(F32), axis=0, keepdims=True)
         d_hidden = dot_nt(g_qkv, weights[:, :QKV_W])
-        grad_mod[pl.ds(step, 1), :D] = jnp.sum(d_hidden, axis=0, keepdims=True)
-        grad_mod[pl.ds(step, 1), D:] = jnp.sum(d_hidden * normed, axis=0, keepdims=True)
+        grad_mod[pl.ds(slot, 1), :D] = jnp.sum(d_hidden, axis=0, keepdims=True)
+        grad_mod[pl.ds(slot, 1), D:] = jnp.sum(d_hidden * normed, axis=0, keepdims=True)
         out[0] = (
-            grad_mid_in[0] + norm_back(d_hidden * (1.0 + row[:, D : 2 * D]), normed, inverse)
+            grad_mid_in[slot] + norm_back(d_hidden * (1.0 + row[:, D : 2 * D]), normed, inverse)
         ).astype(BF)
 
-    @pl.when(step == CAP - 1)
+    if not last:
+        return
+
+    @pl.when(step == CAP - 1 - first)
     def _():
         cond = conditions[...].astype(F32)
         sig = 1.0 / (1.0 + jnp.exp(-cond))
@@ -350,6 +393,10 @@
     return pl.BlockSpec((1, *shape), lambda j, info: (j, *zeros))
 
 
+def held():
+    return pl.BlockSpec(memory_space=pltpu.VMEM)
+
+
 def whole(*shape):
     zeros = (0,) * len(shape)
     return pl.BlockSpec(shape, lambda j, info: zeros)
@@ -367,17 +414,8 @@
         grid_spec=pltpu.PrefetchScalarGridSpec(
             num_scalar_prefetch=1,
             grid=(CAP,),
-            in_specs=[slot_spec(TOK, D), whole(CAP, D)] + [whole(48, LANES_ONE)] * 8,
-            out_specs=[
-                whole(D, LANES_ONE),
-                whole(48, 128),
-                whole(CAP, MOD_ONE),
-                slot_out(TOK, QKV_W),
-                slot_out(HEADS, TOK, TOK),
-                slot_out(TOK, D),
-                slot_out(TOK, D),
-                slot_out(TOK, D),
-            ],
+            in_specs=[slot_spec(TOK, D), whole(CAP, D)] + [held()] * 8,
+            out_specs=[held()] * 8,
         ),
         out_shape=[
             jax.ShapeDtypeStruct((D, LANES_ONE), BF),
@@ -406,20 +444,12 @@
             in_specs=[
                 slot_spec(TOK, D),
                 whole(CAP, D),
+                held(),
                 slot_spec(TOK, D),
-                slot_spec(TOK, D),
-                whole(48, 128),
+                held(),
             ]
-            + [whole(48, LANES_TWO)] * 8,
-            out_specs=[
-                whole(D, LANES_TWO),
-                slot_out(TOK, D),
-                slot_out(TOK, D),
-                slot_out(TOK, D),
-                whole(CAP, MOD_TWO),
-                whole(192, LANES_TWO),
-                whole(192, LANES_TWO),
-            ],
+            + [held()] * 8,
+            out_specs=[held(), slot_out(TOK, D)] + [held()] * 5,
             scratch_shapes=[
                 pltpu.VMEM((CAP, MOD_TWO), F32),
                 pltpu.VMEM((D, FF), F32),
@@ -445,57 +475,41 @@
     )(info, latents, conditions, mixed, grad_out, bias, *pieces)
 
 
-def run_backward(
-    info, latents, conditions, qkv, expo, mixed, rinv, hidden, grad_mid, grad_mixed, mod,
-    weights, weights_two, grad_mod_two,
-):
+def run_backward(first, count, info, latents, shared, carried=None):
+    last = carried is not None
+
+    def slot_at(j, info):
+        return (jnp.minimum(j + first, jnp.maximum(info[0] - 1, 0)), 0, 0)
+
+    in_specs = [pl.BlockSpec((1, TOK, D), slot_at), whole(CAP, D)] + [held()] * 9
+    out_specs = [pl.BlockSpec((1, TOK, D), lambda j, info: (j + first, 0, 0))]
+    out_shape = [jax.ShapeDtypeStruct((CAP, TOK, D), BF)]
+    state = [(D, QKV_W), (8, QKV_W), (CAP, MOD_ONE)]
+    if last:
+        in_specs += [held()] * 5 + [pl.BlockSpec(memory_space=pl.ANY)]
+        out_specs += [whole(CAP, D), held(), held()]
+        out_shape += [jax.ShapeDtypeStruct((CAP, D), BF)]
+        out_shape += [jax.ShapeDtypeStruct((192, LANES_ONE), BF)] * 2
+    else:
+        out_specs += [held()] * 3
+        out_shape += [jax.ShapeDtypeStruct(shape, F32) for shape in state]
     return pl.pallas_call(
-        backward_kernel,
+        functools.partial(backward_kernel, first, last),
         grid_spec=pltpu.PrefetchScalarGridSpec(
             num_scalar_prefetch=1,
-            grid=(CAP,),
-            in_specs=[
-                slot_spec(TOK, D),
-                whole(CAP, D),
-                slot_spec(TOK, QKV_W),
-                slot_spec(HEADS, TOK, TOK),
-                slot_spec(TOK, D),
-                slot_spec(TOK, D),
-                slot_spec(TOK, D),
-                slot_spec(TOK, D),
-                slot_spec(TOK, D),
-                whole(CAP, MOD_ONE),
-                whole(D, LANES_ONE),
-                whole(D, LANES_TWO),
-                whole(CAP, MOD_TWO),
-            ],
-            out_specs=[
-                slot_out(TOK, D),
-                whole(CAP, D),
-                whole(192, LANES_ONE),
-                whole(192, LANES_ONE),
-            ],
-            scratch_shapes=[
-                pltpu.VMEM((D, QKV_W), F32),
-                pltpu.VMEM((8, QKV_W), F32),
-                pltpu.VMEM((CAP, MOD_ONE), F32),
-            ],
+            grid=(count,),
+            in_specs=in_specs,
+            out_specs=out_specs,
+            scratch_shapes=[pltpu.VMEM(shape, F32) for shape in state] if last else [],
         ),
-        out_shape=[
-            jax.ShapeDtypeStruct((CAP, TOK, D), BF),
-            jax.ShapeDtypeStruct((CAP, D), BF),
-            jax.ShapeDtypeStruct((192, LANES_ONE), BF),
-            jax.ShapeDtypeStruct((192, LANES_ONE), BF),
-        ],
+        out_shape=out_shape,
+        input_output_aliases={17: 0} if last else {},
         compiler_params=params(),
-        name="attention_backward",
+        name="attention_backward_rest" if last else "attention_backward_start",
         cost_estimate=pl.CostEstimate(
-            flops=9_000_000_000, bytes_accessed=30_000_000, transcendentals=1_000
+            flops=1_100_000_000 * count, bytes_accessed=4_000_000 * count, transcendentals=1_000
         ),
-    )(
-        info, latents, conditions, qkv, expo, mixed, rinv, hidden, grad_mid, grad_mixed, mod,
-        weights, weights_two, grad_mod_two,
-    )
+    )(info, latents, *shared, *(carried or ()))
 
 
 def place(index):
@@ -533,37 +547,51 @@
     return routes(lambda zh, x, y, zl, c: index_of(zh, x, (y + k) % 4, zl, c))
 
 
-def gather(block):
-    mine = [move(block, fetch(k)) for k in range(4)]
-    other = [move(piece, CORE_SWAP) for piece in mine]
-    return mine + other
+def after(value, *earlier):
+    return lax.optimization_barrier((value, *earlier))[0]
+
+
+def fetch_all(block):
+    return [move(block, fetch(k)) for k in range(4)]
+
+
+def swap_all(pieces):
+    return [move(piece, CORE_SWAP) for piece in pieces]
 
 
 def add(values, dtype=BF):
     return sum(v.astype(F32) for v in values).astype(dtype)
 
 
-def reduce(keep, send):
-    held = add([keep, move(send, CORE_SWAP)])
+def scatter(held_sum):
     arrived = []
     for k in range(4):
         back = [(target, source) for source, target in fetch(k)]
-        arrived.append(move(held[48 * k : 48 * k + 48], back))
+        arrived.append(move(held_sum[48 * k : 48 * k + 48], back))
+    return arrived
+
+
+def sum_replicas(arrived, core):
+    lanes = arrived[0].shape[1] // 2
     total = add(arrived)
-    total = add([total, move(total, CORE_SWAP)])
+    mine = lax.dynamic_slice(total, (0, core * lanes), (48, lanes))
+    other = lax.dynamic_slice(total, (0, (1 - core) * lanes), (48, lanes))
+    total = add([mine, move(other, CORE_SWAP)])
     total = add([total, move(total, ZLOW_SWAP)])
-    return add([total] + [move(total, y_route(k)) for k in (1, 2, 3)], F32)
-
-
-def pack_bias(shard, mod_bias, qv_bias, proj_bias, up_bias, down_bias):
-    flat = jnp.zeros((48 * 128,), BF)
-    qv_at = shard * 96 + jnp.where(shard >= 4, D, 0)
-    flat = lax.dynamic_update_slice(flat, qv_bias, (qv_at,))
-    flat = lax.dynamic_update_slice(flat, mod_bias, (ROW_MOD * 128 + shard * 288,))
-    flat = lax.dynamic_update_slice(flat, proj_bias, (ROW_PROJ * 128 + shard * 48,))
-    flat = lax.dynamic_update_slice(flat, up_bias, (ROW_UP * 128 + shard * 192,))
-    flat = lax.dynamic_update_slice(flat, down_bias, (ROW_DOWN * 128 + shard * 48,))
-    return flat.reshape(48, 128)
+    total = add([total] + [move(total, y_route(k)) for k in (1, 2, 3)])
+    swapped = move(total, CORE_SWAP)
+    halves = [jnp.where(core == 0, total, swapped), jnp.where(core == 0, swapped, total)]
+    return jnp.concatenate(halves, axis=1).astype(F32)
+
+
+def pack_bias(mod_bias, qv_bias, proj_bias, up_bias, down_bias):
+    def whole_rows(value):
+        return jnp.pad(value, (0, -value.shape[0] % 128))
+
+    flat = jnp.concatenate(
+        [whole_rows(v) for v in (qv_bias, mod_bias, proj_bias, up_bias, down_bias)]
+    )
+    return jnp.pad(flat.reshape(8, 128), ((0, 40), (0, 0)))
 
 
 def on_device(
@@ -573,7 +601,7 @@
     shard = lax.axis_index("shard")
     rep = lax.axis_index("rep")
     info = jnp.stack([counts[0], shard % 4, shard // 4, rep % 2]).astype(jnp.int32)
-    biases = pack_bias(shard, mod_bias, qv_bias, proj_bias, up_bias, down_bias)
+    biases = pack_bias(mod_bias, qv_bias, proj_bias, up_bias, down_bias)
     block_one = jnp.concatenate([qkv_weight, mod_weight[:, :MOD_ONE], biases], axis=1)
     block_two = jnp.concatenate(
         [up_weight, mod_weight[:, MOD_ONE:], proj_weight]
@@ -581,20 +609,32 @@
         + [jnp.zeros((48, 128), BF)],
         axis=1,
     )
-    pieces_one = gather(block_one)
-    pieces_two = gather(block_two)
+    core = rep % 2
+    mine_one = fetch_all(block_one)
+    other_one = swap_all(mine_one)
+    mine_two = fetch_all(after(block_two, *mine_one))
     weights, bias, mod, qkv, expo, mixed, rinv, hidden = run_forward(
-        info, latents, conditions, pieces_one
-    )
+        info, latents, conditions, mine_one + other_one
+    )
+    other_two = swap_all(mine_two)
     weights_two, out, grad_mid, grad_mixed, grad_mod_two, keep_two, send_two = run_middle(
-        info, latents, conditions, mixed, grad_out, bias, pieces_two
-    )
+        info, latents, conditions, mixed, grad_out, bias, mine_two + other_two
+    )
+    swapped_two = move(send_two, CORE_SWAP)
+    shared = (
+        conditions, qkv, expo, mixed, rinv, hidden, grad_mid, grad_mixed, mod, weights,
+    )
+    grad_latents, acc_qkv, acc_bias, grad_mod = run_backward(0, 2, info, latents, shared)
+    held_two = add([keep_two, after(swapped_two, acc_bias)])
+    arrived_two = scatter(held_two)
     grad_latents, grad_cond, keep_one, send_one = run_backward(
-        info, latents, conditions, qkv, expo, mixed, rinv, hidden, grad_mid, grad_mixed, mod,
-        weights, weights_two, grad_mod_two,
-    )
-    two = reduce(keep_two, send_two)
-    one = reduce(keep_one, send_one)
+        2, 6, info, latents, shared,
+        (weights_two, grad_mod_two, acc_qkv, acc_bias, after(grad_mod, held_two), grad_latents),
+    )
+    held_one = add([keep_one, move(send_one, CORE_SWAP)])
+    arrived_one = scatter(held_one)
+    two = sum_replicas(arrived_two, core)
+    one = sum_replicas(arrived_one, core)
     grad_bias = (
         one[:, BIAS_ONE : BIAS_ONE + 128] + two[:, BIAS_TWO : BIAS_TWO + 128]
     ).reshape(-1)

time: 248 us -> 251 us (1.012)
  starting transfers between devices: 77.1 us -> 140 us
  waiting for transfers between devices: 74.6 us -> 41.5 us
  Pallas kernels: 70.6 us -> 46 us
    ppermute x36 -> x38, starting transfers between devices: 77.1 us -> 140 us  [move(): return lax.ppermute(value, BOTH, pairs)]
    ppermute x36 -> x38, waiting for transfers between devices: 74.6 us -> 41.5 us  [move(): return lax.ppermute(value, BOTH, pairs)]
    pallas_call x1, Pallas kernels: 35.4 us -> 12.2 us  [run_middle(): pl.pallas_call(middle_kernel, grid_spec=pltpu.PrefetchScalarGridSpec(num_...]
    dynamic_update_slice x5 -> x0, local copies, waits for them, and re-layouts: 4.21 us -> none  [the longest x1 0.86 us: pack_bias(): lax.dynamic_update_slice(flat, mod_bias, (ROW_MOD * 128 + shard * 288,))]
    pallas_call x1, Pallas kernels: 13.4 us -> 9.44 us  [run_forward(): pl.pallas_call(forward_kernel, grid_spec=pltpu.PrefetchScalarGridSpec(num...]
    pad x0 -> x5, local copies, waits for them, and re-layouts: none -> 3.32 us  [whole_rows(): return jnp.pad(value, (0, -value.shape[0] % 128))]
    pallas_call x1 -> x2, Pallas kernels: 21.8 us -> 24.4 us  [run_backward(): pl.pallas_call(functools.partial(backward_kernel, first, last), grid_spec...]
    unnamed x35 -> x41, local copies, waits for them, and re-layouts: 7.62 us -> 7.58 us
  transfers between devices with their start and end apart: 36 -> 38, of which waited for: 16 -> 16; matrix products, arithmetic and copies ran while one was open for 4% -> 3% of each run, Pallas kernels for 14% -> 8%
where the time goes in v2:
time: 251 us
  starting transfers between devices  140 us (56%)
  Pallas kernels  46 us (18%)
  waiting for transfers between devices  41.5 us (17%)
  local copies, waits for them, and re-layouts  16.2 us (6%)
  other arithmetic  5.54 us (2%)
    ppermute x38, starting transfers between devices, move(): return lax.ppermute(value, BOTH, pairs)  140 us
    ppermute x38, waiting for transfers between devices, move(): return lax.ppermute(value, BOTH, pairs)  41.5 us
    pallas_call x2, Pallas kernels, run_backward(): pl.pallas_call(functools.partial(backward_kernel, first, last), grid_spec...  24.4 us
    pallas_call x1, Pallas kernels, run_middle(): pl.pallas_call(middle_kernel, grid_spec=pltpu.PrefetchScalarGridSpec(num_...  12.2 us
    pallas_call x1, Pallas kernels, run_forward(): pl.pallas_call(forward_kernel, grid_spec=pltpu.PrefetchScalarGridSpec(num...  9.44 us
    unnamed x41, local copies, waits for them, and re-layouts  7.58 us
  transfers between devices with their start and end apart: 38, of which 16 were waited for; matrix products, arithmetic and copies ran while one was open for 3% of the time, Pallas kernels for 8%

profile of v2, /device:TPU:1, one launch (start us, length us, event | category | flops | bytes accessed | tf_op | source)
XLA Modules:
  0.0 251.1 jit_solution(11576563417076130487)
XLA Ops:
  6.7 5.6 %collective-permute-start.3 = (bf16[48,2048]{1,0:T(8,128)(2,1)S(1)}, bf16[48,2048]{1,0:T(8,128)(2,1)S(1)}, u32[]{:S(2)}, u32[]{:S(2)}) collective-permute-start(bf16[48,2048]{1,0:T(8,128)(2,1)S(1)} %fusion.1), channel_id=1, source_target_pairs={{48,0},{115,1},{50,2},{113,3},{52,4},{119,5},{54,6},{117,7},{56,8}... | collective-permute-start | bytes 589832 | tf_op jit(solution)/shard_map/ppermute | solution.py:543
  13.9 4.1 %collective-permute-start.1 = (bf16[48,2048]{1,0:T(8,128)(2,1)S(1)}, bf16[48,2048]{1,0:T(8,128)(2,1)S(1)}, u32[]{:S(2)}, u32[]{:S(2)}) collective-permute-start(bf16[48,2048]{1,0:T(8,128)(2,1)S(1)} %fusion.1), channel_id=1, source_target_pairs={{16,0},{83,1},{18,2},{81,3},{20,4},{87,5},{22,6},{85,7},{24,8},{91... | collective-permute-start | bytes 589832 | tf_op jit(solution)/shard_map/ppermute | solution.py:543
  33.2 3.9 %collective-permute-start.8 = (bf16[48,5120]{1,0:T(8,128)(2,1)S(1)}, bf16[48,5120]{1,0:T(8,128)(2,1)S(1)}, u32[]{:S(2)}, u32[]{:S(2)}) collective-permute-start(bf16[48,5120]{1,0:T(8,128)(2,1)S(1)} %constant_dynamic-update-slice_fusion), channel_id=1, source_target_pairs={{0,0},{67,1},{2,2},{65,3},{4,4},{71,5},{6,6},{69,7},{8,8},{75,9},{... | collective-permute-start | bytes 1474568 | tf_op jit(solution)/shard_map/ppermute | solution.py:543
  38.8 15.2 %collective-permute-done.11.p3 = bf16[48,5120]{1,0:T(8,128)(2,1)S(1)} collective-permute-done((bf16[48,5120]{1,0:T(8,128)(2,1)S(1)}, bf16[48,5120]{1,0:T(8,128)(2,1)S(1)}, u32[]{:S(2)}, u32[]{:S(2)}) %collective-permute-start.11) | collective-permute-done | bytes 491552 | tf_op jit(solution)/shard_map/ppermute | solution.py:543
  59.1 9.4 %attention_forward.1 = (bf16[384,2048]{1,0:T(8,128)(2,1)}, f32[48,128]{1,0:T(8,128)}, f32[8,768]{1,0:T(8,128)}, bf16[8,256,1152]{2,1,0:T(8,128)(2,1)}, bf16[8,6,...) custom-call(s32[4]{0:T(128)} %pad_add_fusion.info, ...), custom_call_target="tpu_custom_call" | custom-call | flops 3000000000 | bytes 20000000 | tf_op jit(solution)/shard_map/attention_forward/pallas_call | solution.py:412
  69.7 12.2 %feed_forward_both_ways.1 = (bf16[384,5120]{1,0:T(8,128)(2,1)}, bf16[8,256,384]{2,1,0:T(8,128)(2,1)}, f32[8,256,384]{2,1,0:T(8,128)}, bf16[8,256,384]{2,1,0:T(8,...) custom-call(s32[4]{0:T(128)} %pad_add_fusion.info, ...), custom_call_target="tpu_custom_call" | custom-call | flops 16000000000 | bytes 30000000 | tf_op jit(solution)/shard_map/feed_forward_both_ways/pallas_call | solution.py:439
  81.9 31.5 %collective-permute-start.16 = (bf16[192,5120]{1,0:T(8,128)(2,1)}, bf16[192,5120]{1,0:T(8,128)(2,1)S(1)}, u32[]{:S(2)}, u32[]{:S(2)}) collective-permute-start(bf16[192,5120]{1,0:T(8,128)(2,1)} %get-tuple-element.57), channel_id=1, source_target_pairs={{0,1},{1,0},{2,3},{3,2},{4,5},{5,4},{6,7},{7,6},{8,9},{9,8},{10,11... | collective-permute-start | bytes 5898248 | tf_op jit(solution)/shard_map/ppermute | solution.py:543
  113.4 10.3 %attention_backward_start.1 = (bf16[8,256,384]{2,1,0:T(8,128)(2,1)}, f32[384,1152]{1,0:T(8,128)}, f32[8,1152]{1,0:T(8,128)}, f32[8,768]{1,0:T(8,128)}) custom-call(s32[4]{0:T(128)} %pad_add_fusion.info, bf16[8,256,384]{2,1,0:T(8,128)(2,1)} %latents.7, bf16[8,384]{1,0:T(8,128)(2,1)} %conditions.7, bf16[8,256,1152]{2,1,0:T(8,128)(2,1)} %get-tuple-element.43.qkv_in, ...), custom_call_target="tpu_custom_call" | custom-call | flops 2200000000 | bytes 8000000 | tf_op jit(solution)/shard_map/attention_backward_start/pallas_call | solution.py:496
  124.3 14.1 %attention_backward_rest.1 = (bf16[8,256,384]{2,1,0:T(8,128)(2,1)}, bf16[8,384]{1,0:T(8,128)(2,1)}, bf16[192,2048]{1,0:T(8,128)(2,1)}, bf16[192,2048]{1,0:T(8,128)(2,1)}) custom-call(s32[4]{0:T(128)} %pad_add_fusion.info, bf16[8,256,384]{2,1,0:T(8,128)(2,1)} %latents.7, bf16[8,384]{1,0:T(8,128)(2,1)} %conditions.7, ...), custom_call_target="tpu_custom_call", output_to_operand_aliasing={{0}: (17, {})} | custom-call | flops 6600000000 | bytes 24000000 | tf_op jit(solution)/shard_map/attention_backward_rest/pallas_call | solution.py:496
  138.4 13.1 %collective-permute-start.17 = (bf16[192,2048]{1,0:T(8,128)(2,1)}, bf16[192,2048]{1,0:T(8,128)(2,1)S(1)}, u32[]{:S(2)}, u32[]{:S(2)}) collective-permute-start(bf16[192,2048]{1,0:T(8,128)(2,1)} %get-tuple-element.64), channel_id=1, source_target_pairs={{0,1},{1,0},{2,3},{3,2},{4,5},{5,4},{6,7},{7,6},{8,9},{9,8},{10,11... | collective-permute-start | bytes 2359304 | tf_op jit(solution)/shard_map/ppermute | solution.py:543
  151.7 13.4 %collective-permute-start.28 = (bf16[48,5120]{1,0:T(8,128)(2,1)S(1)}, bf16[48,5120]{1,0:T(8,128)(2,1)S(1)}, u32[]{:S(2)}, u32[]{:S(2)}) collective-permute-start(bf16[48,5120]{1,0:T(8,128)(2,1)S(1)} %get-tuple-element.65), channel_id=1, source_target_pairs={{0,0},{1,67},{2,2},{3,65},{4,4},{5,71},{6,6},{7,69},{8,8},{9,75},{... | collective-permute-start | bytes 1474568 | tf_op jit(solution)/shard_map/ppermute | solution.py:543
  165.1 9.3 %collective-permute-start.31 = (bf16[48,5120]{1,0:T(8,128)(2,1)S(1)}, bf16[48,5120]{1,0:T(8,128)(2,1)S(1)}, u32[]{:S(2)}, u32[]{:S(2)}) collective-permute-start(bf16[48,5120]{1,0:T(8,128)(2,1)S(1)} %get-tuple-element.66), channel_id=1, source_target_pairs={{0,48},{1,115},{2,50},{3,113},{4,52},{5,119},{6,54},{7,117},{8,56}... | collective-permute-start | bytes 1474568 | tf_op jit(solution)/shard_map/ppermute | solution.py:543
  174.4 9.1 %collective-permute-start.30 = (bf16[48,5120]{1,0:T(8,128)(2,1)S(1)}, bf16[48,5120]{1,0:T(8,128)(2,1)S(1)}, u32[]{:S(2)}, u32[]{:S(2)}) collective-permute-start(bf16[48,5120]{1,0:T(8,128)(2,1)S(1)} %get-tuple-element.67), channel_id=1, source_target_pairs={{0,32},{1,99},{2,34},{3,97},{4,36},{5,103},{6,38},{7,101},{8,40},{... | collective-permute-start | bytes 1474568 | tf_op jit(solution)/shard_map/ppermute | solution.py:543
  183.9 3.7 %collective-permute-start.18 = (bf16[48,2048]{1,0:T(8,128)(2,1)S(1)}, bf16[48,2048]{1,0:T(8,128)(2,1)S(1)}, u32[]{:S(2)}, u32[]{:S(2)}) collective-permute-start(bf16[48,2048]{1,0:T(8,128)(2,1)S(1)} %get-tuple-element.71), channel_id=1, source_target_pairs={{0,0},{1,67},{2,2},{3,65},{4,4},{5,71},{6,6},{7,69},{8,8},{9,75},{... | collective-permute-start | bytes 589832 | tf_op jit(solution)/shard_map/ppermute | solution.py:543
  187.6 4.8 %collective-permute-start.21 = (bf16[48,2048]{1,0:T(8,128)(2,1)S(1)}, bf16[48,2048]{1,0:T(8,128)(2,1)S(1)}, u32[]{:S(2)}, u32[]{:S(2)}) collective-permute-start(bf16[48,2048]{1,0:T(8,128)(2,1)S(1)} %get-tuple-element.72), channel_id=1, source_target_pairs={{0,48},{1,115},{2,50},{3,113},{4,52},{5,119},{6,54},{7,117},{8,56}... | collective-permute-start | bytes 589832 | tf_op jit(solution)/shard_map/ppermute | solution.py:543
  193.5 10.7 %collective-permute-start.20 = (bf16[48,2048]{1,0:T(8,128)(2,1)S(1)}, bf16[48,2048]{1,0:T(8,128)(2,1)S(1)}, u32[]{:S(2)}, u32[]{:S(2)}) collective-permute-start(bf16[48,2048]{1,0:T(8,128)(2,1)S(1)} %get-tuple-element.73), channel_id=1, source_target_pairs={{0,32},{1,99},{2,34},{3,97},{4,36},{5,103},{6,38},{7,101},{8,40},{... | collective-permute-start | bytes 589832 | tf_op jit(solution)/shard_map/ppermute | solution.py:543
  204.2 2.8 %collective-permute-start.19 = (bf16[48,2048]{1,0:T(8,128)(2,1)S(1)}, bf16[48,2048]{1,0:T(8,128)(2,1)S(1)}, u32[]{:S(2)}, u32[]{:S(2)}) collective-permute-start(bf16[48,2048]{1,0:T(8,128)(2,1)S(1)} %get-tuple-element.74), channel_id=1, source_target_pairs={{0,16},{1,83},{2,18},{3,81},{4,20},{5,87},{6,22},{7,85},{8,24},{9,... | collective-permute-start | bytes 589832 | tf_op jit(solution)/shard_map/ppermute | solution.py:543
  209.5 3.2 %collective-permute-done.19 = bf16[48,2048]{1,0:T(8,128)(2,1)S(1)} collective-permute-done((bf16[48,2048]{1,0:T(8,128)(2,1)S(1)}, bf16[48,2048]{1,0:T(8,128)(2,1)S(1)}, u32[]{:S(2)}, u32[]{:S(2)}) %collective-permute-start.19) | collective-permute-done | bytes 196640 | tf_op jit(solution)/shard_map/ppermute | solution.py:543
  215.9 2.6 %collective-permute-done.23 = bf16[48,1024]{1,0:T(8,128)(2,1)S(1)} collective-permute-done((bf16[48,1024]{1,0:T(8,128)(2,1)S(1)}, bf16[48,1024]{1,0:T(8,128)(2,1)S(1)}, u32[]{:S(2)}, u32[]{:S(2)}) %collective-permute-start.23) | collective-permute-done | bytes 98336 | tf_op jit(solution)/shard_map/ppermute | solution.py:543
  218.6 5.2 %collective-permute-start.26 = (bf16[48,1024]{1,0:T(8,128)(2,1)S(1)}, bf16[48,1024]{1,0:T(8,128)(2,1)S(1)}, u32[]{:S(2)}, u32[]{:S(2)}) collective-permute-start(bf16[48,1024]{1,0:T(8,128)(2,1)S(1)} %add_convert_fusion.8), channel_id=1, source_target_pairs={{0,12},{1,13},{2,14},{3,15},{4,0},{5,1},{6,2},{7,3},{8,4},{9,5},{1... | collective-permute-start | bytes 294920 | tf_op jit(solution)/shard_map/ppermute | solution.py:543
  225.1 4.0 %collective-permute-start.36 = (bf16[48,2560]{1,0:T(8,128)(2,1)S(1)}, bf16[48,2560]{1,0:T(8,128)(2,1)S(1)}, u32[]{:S(2)}, u32[]{:S(2)}) collective-permute-start(bf16[48,2560]{1,0:T(8,128)(2,1)S(1)} %add_convert_fusion.4), channel_id=1, source_target_pairs={{0,12},{1,13},{2,14},{3,15},{4,0},{5,1},{6,2},{7,3},{8,4},{9,5},{1... | collective-permute-start | bytes 737288 | tf_op jit(solution)/shard_map/ppermute | solution.py:543
  230.4 2.6 %collective-permute-start.27 = (bf16[48,1024]{1,0:T(8,128)(2,1)S(1)}, bf16[48,1024]{1,0:T(8,128)(2,1)S(1)}, u32[]{:S(2)}, u32[]{:S(2)}) collective-permute-start(bf16[48,1024]{1,0:T(8,128)(2,1)S(1)} %add_convert_fusion.7), channel_id=1, source_target_pairs={{0,1},{1,0},{2,3},{3,2},{4,5},{5,4},{6,7},{7,6},{8,9},{9,8},{10,11... | collective-permute-start | bytes 294920 | tf_op jit(solution)/shard_map/ppermute | solution.py:543
  232.9 6.1 %collective-permute-done.36 = bf16[48,2560]{1,0:T(8,128)(2,1)S(1)} collective-permute-done((bf16[48,2560]{1,0:T(8,128)(2,1)S(1)}, bf16[48,2560]{1,0:T(8,128)(2,1)S(1)}, u32[]{:S(2)}, u32[]{:S(2)}) %collective-permute-start.36) | collective-permute-done | bytes 245792 | tf_op jit(solution)/shard_map/ppermute | solution.py:543
  239.0 4.7 %collective-permute-done.34 = bf16[48,2560]{1,0:T(8,128)(2,1)S(1)} collective-permute-done((bf16[48,2560]{1,0:T(8,128)(2,1)S(1)}, bf16[48,2560]{1,0:T(8,128)(2,1)S(1)}, u32[]{:S(2)}, u32[]{:S(2)}) %collective-permute-start.34) | collective-permute-done | bytes 245792 | tf_op jit(solution)/shard_map/ppermute | solution.py:543
  (137 shorter events, 47.7 us)
Async XLA Ops:
  6.7 19.0 %collective-permute-start.3 = (bf16[48,2048]{1,0:T(8,128)(2,1)S(1)}, bf16[48,2048]{1,0:T(8,128)(2,1)S(1)}, u32[]{:S(2)}, u32[]{:S(2)}) collective-permute-start(bf16[48,2048]{1,0:T(8,128)(2,1)S(1)} %fusion.1), channel_id=1, source_target_pairs={{48,0},{115,1},{50,2},{113,3},{52,4},{119,5},{54,6},{117,7},{56,8}... | collective-permute-start | bytes 589832 | tf_op jit(solution)/shard_map/ppermute | solution.py:543
  12.3 13.5 %collective-permute-start.2 = (bf16[48,2048]{1,0:T(8,128)(2,1)S(1)}, bf16[48,2048]{1,0:T(8,128)(2,1)S(1)}, u32[]{:S(2)}, u32[]{:S(2)}) collective-permute-start(bf16[48,2048]{1,0:T(8,128)(2,1)S(1)} %fusion.1), channel_id=1, source_target_pairs={{32,0},{99,1},{34,2},{97,3},{36,4},{103,5},{38,6},{101,7},{40,8},{... | collective-permute-start | bytes 589832 | tf_op jit(solution)/shard_map/ppermute | solution.py:543
  13.9 11.9 %collective-permute-start.1 = (bf16[48,2048]{1,0:T(8,128)(2,1)S(1)}, bf16[48,2048]{1,0:T(8,128)(2,1)S(1)}, u32[]{:S(2)}, u32[]{:S(2)}) collective-permute-start(bf16[48,2048]{1,0:T(8,128)(2,1)S(1)} %fusion.1), channel_id=1, source_target_pairs={{16,0},{83,1},{18,2},{81,3},{20,4},{87,5},{22,6},{85,7},{24,8},{91... | collective-permute-start | bytes 589832 | tf_op jit(solution)/shard_map/ppermute | solution.py:543
  26.9 27.1 %collective-permute-start.11 = (bf16[48,5120]{1,0:T(8,128)(2,1)S(1)}, bf16[48,5120]{1,0:T(8,128)(2,1)S(1)}, u32[]{:S(2)}, u32[]{:S(2)}) collective-permute-start(bf16[48,5120]{1,0:T(8,128)(2,1)S(1)} %constant_dynamic-update-slice_fusion), channel_id=1, source_target_pairs={{48,0},{115,1},{50,2},{113,3},{52,4},{119,5},{54,6},{117,7},{56,8}... | collective-permute-start | bytes 1474568 | tf_op jit(solution)/shard_map/ppermute | solution.py:543
  28.6 25.4 %collective-permute-start.10 = (bf16[48,5120]{1,0:T(8,128)(2,1)S(1)}, bf16[48,5120]{1,0:T(8,128)(2,1)S(1)}, u32[]{:S(2)}, u32[]{:S(2)}) collective-permute-start(bf16[48,5120]{1,0:T(8,128)(2,1)S(1)} %constant_dynamic-update-slice_fusion), channel_id=1, source_target_pairs={{32,0},{99,1},{34,2},{97,3},{36,4},{103,5},{38,6},{101,7},{40,8},{... | collective-permute-start | bytes 1474568 | tf_op jit(solution)/shard_map/ppermute | solution.py:543
  31.0 24.1 %collective-permute-start.9 = (bf16[48,5120]{1,0:T(8,128)(2,1)S(1)}, bf16[48,5120]{1,0:T(8,128)(2,1)S(1)}, u32[]{:S(2)}, u32[]{:S(2)}) collective-permute-start(bf16[48,5120]{1,0:T(8,128)(2,1)S(1)} %constant_dynamic-update-slice_fusion), channel_id=1, source_target_pairs={{16,0},{83,1},{18,2},{81,3},{20,4},{87,5},{22,6},{85,7},{24,8},{91... | collective-permute-start | bytes 1474568 | tf_op jit(solution)/shard_map/ppermute | solution.py:543
  33.2 23.4 %collective-permute-start.8 = (bf16[48,5120]{1,0:T(8,128)(2,1)S(1)}, bf16[48,5120]{1,0:T(8,128)(2,1)S(1)}, u32[]{:S(2)}, u32[]{:S(2)}) collective-permute-start(bf16[48,5120]{1,0:T(8,128)(2,1)S(1)} %constant_dynamic-update-slice_fusion), channel_id=1, source_target_pairs={{0,0},{67,1},{2,2},{65,3},{4,4},{71,5},{6,6},{69,7},{8,8},{75,9},{... | collective-permute-start | bytes 1474568 | tf_op jit(solution)/shard_map/ppermute | solution.py:543
  38.6 18.0 %collective-permute-start.5 = (bf16[48,2048]{1,0:T(8,128)(2,1)S(1)}, bf16[48,2048]{1,0:T(8,128)(2,1)S(1)}, u32[]{:S(2)}, u32[]{:S(2)}) collective-permute-start(bf16[48,2048]{1,0:T(8,128)(2,1)S(1)} %collective-permute-done.1.p1), channel_id=1, source_target_pairs={{0,1},{1,0},{2,3},{3,2},{4,5},{5,4},{6,7},{7,6},{8,9},{9,8},{10,11... | collective-permute-start | bytes 589832 | tf_op jit(solution)/shard_map/ppermute | solution.py:543
  54.0 14.6 %collective-permute-start.15 = (bf16[48,5120]{1,0:T(8,128)(2,1)S(1)}, bf16[48,5120]{1,0:T(8,128)(2,1)S(1)}, u32[]{:S(2)}, u32[]{:S(2)}) collective-permute-start(bf16[48,5120]{1,0:T(8,128)(2,1)S(1)} %collective-permute-done.11.p3), channel_id=1, source_target_pairs={{0,1},{1,0},{2,3},{3,2},{4,5},{5,4},{6,7},{7,6},{8,9},{9,8},{10,11... | collective-permute-start | bytes 1474568 | tf_op jit(solution)/shard_map/ppermute | solution.py:543
  54.0 14.6 %collective-permute-start.14 = (bf16[48,5120]{1,0:T(8,128)(2,1)S(1)}, bf16[48,5120]{1,0:T(8,128)(2,1)S(1)}, u32[]{:S(2)}, u32[]{:S(2)}) collective-permute-start(bf16[48,5120]{1,0:T(8,128)(2,1)S(1)} %collective-permute-done.10.p2), channel_id=1, source_target_pairs={{0,1},{1,0},{2,3},{3,2},{4,5},{5,4},{6,7},{7,6},{8,9},{9,8},{10,11... | collective-permute-start | bytes 1474568 | tf_op jit(solution)/shard_map/ppermute | solution.py:543
  55.2 13.5 %collective-permute-start.13 = (bf16[48,5120]{1,0:T(8,128)(2,1)S(1)}, bf16[48,5120]{1,0:T(8,128)(2,1)S(1)}, u32[]{:S(2)}, u32[]{:S(2)}) collective-permute-start(bf16[48,5120]{1,0:T(8,128)(2,1)S(1)} %collective-permute-done.9.p1), channel_id=1, source_target_pairs={{0,1},{1,0},{2,3},{3,2},{4,5},{5,4},{6,7},{7,6},{8,9},{9,8},{10,11... | collective-permute-start | bytes 1474568 | tf_op jit(solution)/shard_map/ppermute | solution.py:543
  56.6 12.0 %collective-permute-start.12 = (bf16[48,5120]{1,0:T(8,128)(2,1)S(1)}, bf16[48,5120]{1,0:T(8,128)(2,1)}, u32[]{:S(2)}, u32[]{:S(2)}) collective-permute-start(bf16[48,5120]{1,0:T(8,128)(2,1)S(1)} %collective-permute-done.8.p0), channel_id=1, source_target_pairs={{0,1},{1,0},{2,3},{3,2},{4,5},{5,4},{6,7},{7,6},{8,9},{9,8},{10,11... | collective-permute-start | bytes 1474568 | tf_op jit(solution)/shard_map/ppermute | solution.py:543
  81.9 41.7 %collective-permute-start.16 = (bf16[192,5120]{1,0:T(8,128)(2,1)}, bf16[192,5120]{1,0:T(8,128)(2,1)S(1)}, u32[]{:S(2)}, u32[]{:S(2)}) collective-permute-start(bf16[192,5120]{1,0:T(8,128)(2,1)} %get-tuple-element.57), channel_id=1, source_target_pairs={{0,1},{1,0},{2,3},{3,2},{4,5},{5,4},{6,7},{7,6},{8,9},{9,8},{10,11... | collective-permute-start | bytes 5898248 | tf_op jit(solution)/shard_map/ppermute | solution.py:543
  138.4 45.0 %collective-permute-start.17 = (bf16[192,2048]{1,0:T(8,128)(2,1)}, bf16[192,2048]{1,0:T(8,128)(2,1)S(1)}, u32[]{:S(2)}, u32[]{:S(2)}) collective-permute-start(bf16[192,2048]{1,0:T(8,128)(2,1)} %get-tuple-element.64), channel_id=1, source_target_pairs={{0,1},{1,0},{2,3},{3,2},{4,5},{5,4},{6,7},{7,6},{8,9},{9,8},{10,11... | collective-permute-start | bytes 2359304 | tf_op jit(solution)/shard_map/ppermute | solution.py:543
  151.7 35.9 %collective-permute-start.28 = (bf16[48,5120]{1,0:T(8,128)(2,1)S(1)}, bf16[48,5120]{1,0:T(8,128)(2,1)S(1)}, u32[]{:S(2)}, u32[]{:S(2)}) collective-permute-start(bf16[48,5120]{1,0:T(8,128)(2,1)S(1)} %get-tuple-element.65), channel_id=1, source_target_pairs={{0,0},{1,67},{2,2},{3,65},{4,4},{5,71},{6,6},{7,69},{8,8},{9,75},{... | collective-permute-start | bytes 1474568 | tf_op jit(solution)/shard_map/ppermute | solution.py:543
  165.1 28.4 %collective-permute-start.31 = (bf16[48,5120]{1,0:T(8,128)(2,1)S(1)}, bf16[48,5120]{1,0:T(8,128)(2,1)S(1)}, u32[]{:S(2)}, u32[]{:S(2)}) collective-permute-start(bf16[48,5120]{1,0:T(8,128)(2,1)S(1)} %get-tuple-element.66), channel_id=1, source_target_pairs={{0,48},{1,115},{2,50},{3,113},{4,52},{5,119},{6,54},{7,117},{8,56}... | collective-permute-start | bytes 1474568 | tf_op jit(solution)/shard_map/ppermute | solution.py:543
  174.4 29.8 %collective-permute-start.30 = (bf16[48,5120]{1,0:T(8,128)(2,1)S(1)}, bf16[48,5120]{1,0:T(8,128)(2,1)S(1)}, u32[]{:S(2)}, u32[]{:S(2)}) collective-permute-start(bf16[48,5120]{1,0:T(8,128)(2,1)S(1)} %get-tuple-element.67), channel_id=1, source_target_pairs={{0,32},{1,99},{2,34},{3,97},{4,36},{5,103},{6,38},{7,101},{8,40},{... | collective-permute-start | bytes 1474568 | tf_op jit(solution)/shard_map/ppermute | solution.py:543
  183.5 23.5 %collective-permute-start.29 = (bf16[48,5120]{1,0:T(8,128)(2,1)S(1)}, bf16[48,5120]{1,0:T(8,128)(2,1)S(1)}, u32[]{:S(2)}, u32[]{:S(2)}) collective-permute-start(bf16[48,5120]{1,0:T(8,128)(2,1)S(1)} %get-tuple-element.68), channel_id=1, source_target_pairs={{0,16},{1,83},{2,18},{3,81},{4,20},{5,87},{6,22},{7,85},{8,24},{9,... | collective-permute-start | bytes 1474568 | tf_op jit(solution)/shard_map/ppermute | solution.py:543
  183.9 23.3 %collective-permute-start.18 = (bf16[48,2048]{1,0:T(8,128)(2,1)S(1)}, bf16[48,2048]{1,0:T(8,128)(2,1)S(1)}, u32[]{:S(2)}, u32[]{:S(2)}) collective-permute-start(bf16[48,2048]{1,0:T(8,128)(2,1)S(1)} %get-tuple-element.71), channel_id=1, source_target_pairs={{0,0},{1,67},{2,2},{3,65},{4,4},{5,71},{6,6},{7,69},{8,8},{9,75},{... | collective-permute-start | bytes 589832 | tf_op jit(solution)/shard_map/ppermute | solution.py:543
  187.6 19.7 %collective-permute-start.21 = (bf16[48,2048]{1,0:T(8,128)(2,1)S(1)}, bf16[48,2048]{1,0:T(8,128)(2,1)S(1)}, u32[]{:S(2)}, u32[]{:S(2)}) collective-permute-start(bf16[48,2048]{1,0:T(8,128)(2,1)S(1)} %get-tuple-element.72), channel_id=1, source_target_pairs={{0,48},{1,115},{2,50},{3,113},{4,52},{5,119},{6,54},{7,117},{8,56}... | collective-permute-start | bytes 589832 | tf_op jit(solution)/shard_map/ppermute | solution.py:543
  193.5 16.0 %collective-permute-start.20 = (bf16[48,2048]{1,0:T(8,128)(2,1)S(1)}, bf16[48,2048]{1,0:T(8,128)(2,1)S(1)}, u32[]{:S(2)}, u32[]{:S(2)}) collective-permute-start(bf16[48,2048]{1,0:T(8,128)(2,1)S(1)} %get-tuple-element.73), channel_id=1, source_target_pairs={{0,32},{1,99},{2,34},{3,97},{4,36},{5,103},{6,38},{7,101},{8,40},{... | collective-permute-start | bytes 589832 | tf_op jit(solution)/shard_map/ppermute | solution.py:543
  225.1 14.0 %collective-permute-start.36 = (bf16[48,2560]{1,0:T(8,128)(2,1)S(1)}, bf16[48,2560]{1,0:T(8,128)(2,1)S(1)}, u32[]{:S(2)}, u32[]{:S(2)}) collective-permute-start(bf16[48,2560]{1,0:T(8,128)(2,1)S(1)} %add_convert_fusion.4), channel_id=1, source_target_pairs={{0,12},{1,13},{2,14},{3,15},{4,0},{5,1},{6,2},{7,3},{8,4},{9,5},{1... | collective-permute-start | bytes 737288 | tf_op jit(solution)/shard_map/ppermute | solution.py:543
  229.5 14.2 %collective-permute-start.34 = (bf16[48,2560]{1,0:T(8,128)(2,1)S(1)}, bf16[48,2560]{1,0:T(8,128)(2,1)S(1)}, u32[]{:S(2)}, u32[]{:S(2)}) collective-permute-start(bf16[48,2560]{1,0:T(8,128)(2,1)S(1)} %add_convert_fusion.4), channel_id=1, source_target_pairs={{0,4},{1,5},{2,6},{3,7},{4,8},{5,9},{6,10},{7,11},{8,12},{9,13},{1... | collective-permute-start | bytes 737288 | tf_op jit(solution)/shard_map/ppermute | solution.py:543
  230.4 14.1 %collective-permute-start.27 = (bf16[48,1024]{1,0:T(8,128)(2,1)S(1)}, bf16[48,1024]{1,0:T(8,128)(2,1)S(1)}, u32[]{:S(2)}, u32[]{:S(2)}) collective-permute-start(bf16[48,1024]{1,0:T(8,128)(2,1)S(1)} %add_convert_fusion.7), channel_id=1, source_target_pairs={{0,1},{1,0},{2,3},{3,2},{4,5},{5,4},{6,7},{7,6},{8,9},{9,8},{10,11... | collective-permute-start | bytes 294920 | tf_op jit(solution)/shard_map/ppermute | solution.py:543
  (29 other events, 330.2 us)

commit v3 on v2

--- a/solution.py
+++ b/solution.py
@@ -17,7 +17,7 @@
 TWIN = 128
 BF = jnp.bfloat16
 F32 = jnp.float32
-VMEM_BYTES = 56 * 1024 * 1024
+MIB = 1024 * 1024
 
 LANES_ONE = 2048
 QKV_W = 3 * D
@@ -402,10 +402,14 @@
     return pl.BlockSpec(shape, lambda j, info: zeros)
 
 
-def params():
+def params(mib):
     return pltpu.CompilerParams(
-        dimension_semantics=("arbitrary",), vmem_limit_bytes=VMEM_BYTES
+        dimension_semantics=("arbitrary",), vmem_limit_bytes=mib * MIB
     )
+
+
+def stay(value):
+    return pltpu.with_memory_space_constraint(value, pltpu.VMEM)
 
 
 def run_forward(info, latents, conditions, pieces):
@@ -418,16 +422,16 @@
             out_specs=[held()] * 8,
         ),
         out_shape=[
-            jax.ShapeDtypeStruct((D, LANES_ONE), BF),
-            jax.ShapeDtypeStruct((48, 128), F32),
-            jax.ShapeDtypeStruct((CAP, MOD_ONE), F32),
-            jax.ShapeDtypeStruct((CAP, TOK, QKV_W), BF),
-            jax.ShapeDtypeStruct((CAP, HEADS, TOK, TOK), BF),
-            jax.ShapeDtypeStruct((CAP, TOK, D), BF),
-            jax.ShapeDtypeStruct((CAP, TOK, D), F32),
-            jax.ShapeDtypeStruct((CAP, TOK, D), BF),
+            pltpu.VMEM((D, LANES_ONE), BF),
+            pltpu.VMEM((48, 128), F32),
+            pltpu.VMEM((CAP, MOD_ONE), F32),
+            pltpu.VMEM((CAP, TOK, QKV_W), BF),
+            pltpu.VMEM((CAP, HEADS, TOK, TOK), BF),
+            pltpu.VMEM((CAP, TOK, D), BF),
+            pltpu.VMEM((CAP, TOK, D), F32),
+            pltpu.VMEM((CAP, TOK, D), BF),
         ],
-        compiler_params=params(),
+        compiler_params=params(10),
         name="attention_forward",
         cost_estimate=pl.CostEstimate(
             flops=3_000_000_000, bytes_accessed=20_000_000, transcendentals=3_000_000
@@ -459,20 +463,20 @@
             ],
         ),
         out_shape=[
-            jax.ShapeDtypeStruct((D, LANES_TWO), BF),
+            pltpu.VMEM((D, LANES_TWO), BF),
             jax.ShapeDtypeStruct((CAP, TOK, D), BF),
-            jax.ShapeDtypeStruct((CAP, TOK, D), F32),
-            jax.ShapeDtypeStruct((CAP, TOK, D), BF),
-            jax.ShapeDtypeStruct((CAP, MOD_TWO), F32),
-            jax.ShapeDtypeStruct((192, LANES_TWO), BF),
-            jax.ShapeDtypeStruct((192, LANES_TWO), BF),
+            pltpu.VMEM((CAP, TOK, D), F32),
+            pltpu.VMEM((CAP, TOK, D), BF),
+            pltpu.VMEM((CAP, MOD_TWO), F32),
+            pltpu.VMEM((192, LANES_TWO), BF),
+            pltpu.VMEM((192, LANES_TWO), BF),
         ],
-        compiler_params=params(),
+        compiler_params=params(16),
         name="feed_forward_both_ways",
         cost_estimate=pl.CostEstimate(
             flops=16_000_000_000, bytes_accessed=30_000_000, transcendentals=3_000_000
         ),
-    )(info, latents, conditions, mixed, grad_out, bias, *pieces)
+    )(info, latents, conditions, stay(mixed), grad_out, stay(bias), *pieces)
 
 
 def run_backward(first, count, info, latents, shared, carried=None):
@@ -489,10 +493,10 @@
         in_specs += [held()] * 5 + [pl.BlockSpec(memory_space=pl.ANY)]
         out_specs += [whole(CAP, D), held(), held()]
         out_shape += [jax.ShapeDtypeStruct((CAP, D), BF)]
-        out_shape += [jax.ShapeDtypeStruct((192, LANES_ONE), BF)] * 2
+        out_shape += [pltpu.VMEM((192, LANES_ONE), BF)] * 2
     else:
         out_specs += [held()] * 3
-        out_shape += [jax.ShapeDtypeStruct(shape, F32) for shape in state]
+        out_shape += [pltpu.VMEM(shape, F32) for shape in state]
     return pl.pallas_call(
         functools.partial(backward_kernel, first, last),
         grid_spec=pltpu.PrefetchScalarGridSpec(
@@ -504,12 +508,12 @@
         ),
         out_shape=out_shape,
         input_output_aliases={17: 0} if last else {},
-        compiler_params=params(),
+        compiler_params=params(12),
         name="attention_backward_rest" if last else "attention_backward_start",
         cost_estimate=pl.CostEstimate(
             flops=1_100_000_000 * count, bytes_accessed=4_000_000 * count, transcendentals=1_000
         ),
-    )(info, latents, *shared, *(carried or ()))
+    )(info, latents, shared[0], *map(stay, shared[1:]), *map(stay, (carried or ())[:-1]), *(carried or ())[-1:])
 
 
 def place(index):
@@ -580,18 +584,93 @@
     total = add([total, move(total, ZLOW_SWAP)])
     total = add([total] + [move(total, y_route(k)) for k in (1, 2, 3)])
     swapped = move(total, CORE_SWAP)
-    halves = [jnp.where(core == 0, total, swapped), jnp.where(core == 0, swapped, total)]
-    return jnp.concatenate(halves, axis=1).astype(F32)
-
-
-def pack_bias(mod_bias, qv_bias, proj_bias, up_bias, down_bias):
-    def whole_rows(value):
-        return jnp.pad(value, (0, -value.shape[0] % 128))
-
-    flat = jnp.concatenate(
-        [whole_rows(v) for v in (qv_bias, mod_bias, proj_bias, up_bias, down_bias)]
-    )
-    return jnp.pad(flat.reshape(8, 128), ((0, 40), (0, 0)))
+    return [total, swapped]
+
+
+def row_of(ref):
+    size = ref.shape[0]
+    row = ref[...].astype(F32).reshape(1, size)
+    if size % 128:
+        row = jnp.concatenate([row, jnp.zeros((1, -size % 128), F32)], axis=1)
+    return row
+
+
+def pack_one_kernel(qkv, mod, qv_bias, mod_bias, proj_bias, up_bias, down_bias, out):
+    out[:, :QKV_W] = qkv[...]
+    out[:, QKV_W:BIAS_ONE] = mod[:, :MOD_ONE]
+    flat = [row_of(ref) for ref in (qv_bias, mod_bias, proj_bias, up_bias, down_bias)]
+    flat = jnp.concatenate(flat, axis=1)
+    rows = [flat[:, 128 * i : 128 * i + 128] for i in range(8)] + [jnp.zeros((40, 128), F32)]
+    out[:, BIAS_ONE:] = jnp.concatenate(rows, axis=0).astype(BF)
+
+
+def pack_two_kernel(up, mod, proj, down, out):
+    out[:, :FF] = up[...]
+    out[:, AT_MOD:AT_PROJ] = mod[:, MOD_ONE:]
+    out[:, AT_PROJ:AT_DOWN] = proj[...]
+    for q in range(4):
+        out[:, AT_DOWN + D * q : AT_DOWN + D * q + D] = down[48 * q : 48 * q + 48, :]
+    out[:, BIAS_TWO:] = jnp.zeros((48, 128), BF)
+
+
+def pack(kernel, name, lanes, *values):
+    return pl.pallas_call(
+        kernel,
+        out_shape=jax.ShapeDtypeStruct((48, lanes), BF),
+        compiler_params=pltpu.CompilerParams(vmem_limit_bytes=8 * MIB),
+        name=name,
+    )(*values)
+
+
+def finish_kernel(
+    info, one_a, one_b, two_a, two_b, g_mod, g_mod_bias, g_qkv, g_qv_bias, g_proj, g_proj_bias,
+    g_up, g_up_bias, g_down, g_down_bias,
+):
+    shard, first = info[1] + 4 * info[2], info[3] == 0
+
+    def joined(mine, other):
+        mine, other = mine[...].astype(F32), other[...].astype(F32)
+        return jnp.concatenate(
+            [jnp.where(first, mine, other), jnp.where(first, other, mine)], axis=1
+        )
+
+    one, two = joined(one_a, one_b), joined(two_a, two_b)
+    g_mod[:, :MOD_ONE] = one[:, QKV_W:BIAS_ONE]
+    g_mod[:, MOD_ONE:] = two[:, AT_MOD:AT_PROJ]
+    g_qkv[...] = one[:, :QKV_W]
+    g_proj[...] = two[:, AT_PROJ:AT_DOWN]
+    g_up[...] = two[:, :FF]
+    for q in range(4):
+        g_down[48 * q : 48 * q + 48, :] = two[:, AT_DOWN + D * q : AT_DOWN + D * q + D]
+    bias = one[:, BIAS_ONE:] + two[:, BIAS_TWO:]
+
+    def own(first_row, count, size, out):
+        row = bias_row(bias, first_row, count)
+        row = jnp.broadcast_to(row, (8, 128 * count))
+        turn = lax.rem(8 * size - shard * size, 8 * size)
+        out[...] = pltpu.roll(row, turn, 1)[0:1, :size].reshape(size)
+
+    own(ROW_MOD, 18, 288, g_mod_bias)
+    query, value = bias_row(bias, 0, 3), bias_row(bias, 6, 3)
+    row = jnp.broadcast_to(jnp.concatenate([query, value], axis=1), (8, 2 * D))
+    turn = lax.rem(2 * D - shard * 96, 2 * D)
+    g_qv_bias[...] = pltpu.roll(row, turn, 1)[0:1, :96].reshape(96)
+    own(ROW_PROJ, 3, 48, g_proj_bias)
+    own(ROW_UP, 12, 192, g_up_bias)
+    own(ROW_DOWN, 3, 48, g_down_bias)
+
+
+def finish(info, parts):
+    shapes = [
+        (48, 6 * D), (288,), (48, QKV_W), (96,), (48, D), (48,), (48, FF), (192,), (192, D), (48,),
+    ]
+    return pl.pallas_call(
+        finish_kernel,
+        in_specs=[pl.BlockSpec(memory_space=pltpu.SMEM)] + [held()] * 4,
+        out_shape=[jax.ShapeDtypeStruct(shape, F32) for shape in shapes],
+        compiler_params=pltpu.CompilerParams(vmem_limit_bytes=12 * MIB),
+        name="unpack_gradients",
+    )(info, *parts)
 
 
 def on_device(
@@ -601,13 +680,13 @@
     shard = lax.axis_index("shard")
     rep = lax.axis_index("rep")
     info = jnp.stack([counts[0], shard % 4, shard // 4, rep % 2]).astype(jnp.int32)
-    biases = pack_bias(mod_bias, qv_bias, proj_bias, up_bias, down_bias)
-    block_one = jnp.concatenate([qkv_weight, mod_weight[:, :MOD_ONE], biases], axis=1)
-    block_two = jnp.concatenate(
-        [up_weight, mod_weight[:, MOD_ONE:], proj_weight]
-        + [down_weight[48 * q : 48 * q + 48] for q in range(4)]
-        + [jnp.zeros((48, 128), BF)],
-        axis=1,
+    block_one = pack(
+        pack_one_kernel, "pack_attention_weights", LANES_ONE,
+        qkv_weight, mod_weight, qv_bias, mod_bias, proj_bias, up_bias, down_bias,
+    )
+    block_two = pack(
+        pack_two_kernel, "pack_feed_forward_weights", LANES_TWO,
+        up_weight, mod_weight, proj_weight, down_weight,
     )
     core = rep % 2
     mine_one = fetch_all(block_one)
@@ -616,6 +695,7 @@
     weights, bias, mod, qkv, expo, mixed, rinv, hidden = run_forward(
         info, latents, conditions, mine_one + other_one
     )
+    mine_two = [after(piece, mod) for piece in mine_two]
     other_two = swap_all(mine_two)
     weights_two, out, grad_mid, grad_mixed, grad_mod_two, keep_two, send_two = run_middle(
         info, latents, conditions, mixed, grad_out, bias, mine_two + other_two
@@ -631,33 +711,11 @@
         2, 6, info, latents, shared,
         (weights_two, grad_mod_two, acc_qkv, acc_bias, after(grad_mod, held_two), grad_latents),
     )
-    held_one = add([keep_one, move(send_one, CORE_SWAP)])
+    held_one = add([keep_one, move(after(send_one, *arrived_two), CORE_SWAP)])
     arrived_one = scatter(held_one)
     two = sum_replicas(arrived_two, core)
     one = sum_replicas(arrived_one, core)
-    grad_bias = (
-        one[:, BIAS_ONE : BIAS_ONE + 128] + two[:, BIAS_TWO : BIAS_TWO + 128]
-    ).reshape(-1)
-    qv_at = shard * 96 + jnp.where(shard >= 4, D, 0)
-
-    def part(first, size):
-        return lax.dynamic_slice(grad_bias, (first,), (size,))
-
-    return (
-        out,
-        grad_latents,
-        grad_cond,
-        jnp.concatenate([one[:, QKV_W : QKV_W + MOD_ONE], two[:, AT_MOD : AT_MOD + MOD_TWO]], 1),
-        part(ROW_MOD * 128 + shard * 288, 288),
-        one[:, :QKV_W],
-        part(qv_at, 96),
-        two[:, AT_PROJ : AT_PROJ + D],
-        part(ROW_PROJ * 128 + shard * 48, 48),
-        two[:, :FF],
-        part(ROW_UP * 128 + shard * 192, 192),
-        jnp.concatenate([two[:, AT_DOWN + D * q : AT_DOWN + D * q + D] for q in range(4)], 0),
-        part(ROW_DOWN * 128 + shard * 48, 48),
-    )
+    return (out, grad_latents, grad_cond, *finish(info, one + two))
 
 
 def solution(mesh):

time: 251 us -> 230 us (0.916)
  local copies, waits for them, and re-layouts: 16.2 us -> 48.3 us
  starting transfers between devices: 140 us -> 110 us
  Pallas kernels: 46 us -> 16.3 us
  waiting for transfers between devices: 41.5 us -> 48.4 us
    unnamed x41 -> x108, local copies, waits for them, and re-layouts: 7.58 us -> 48 us
    ppermute x38, starting transfers between devices: 140 us -> 110 us  [move(): return lax.ppermute(value, BOTH, pairs)]
    pallas_call x2, Pallas kernels: 24.4 us -> 5.28 us  [run_backward(): pl.pallas_call(functools.partial(backward_kernel, first, last), grid_spec...]
    pallas_call x1, Pallas kernels: 9.44 us -> 1.09 us  [run_forward(): pl.pallas_call(forward_kernel, grid_spec=pltpu.PrefetchScalarGridSpec(num...]
    ppermute x38, waiting for transfers between devices: 41.5 us -> 48.4 us  [move(): return lax.ppermute(value, BOTH, pairs)]
    pallas_call x1, Pallas kernels: 12.2 us -> 7.36 us  [run_middle(): pl.pallas_call(middle_kernel, grid_spec=pltpu.PrefetchScalarGridSpec(num_...]
    pad x5 -> x0, local copies, waits for them, and re-layouts: 3.32 us -> none  [whole_rows(): return jnp.pad(value, (0, -value.shape[0] % 128))]
    pallas_call x0 -> x3, Pallas kernels: none -> 2.57 us  [the longest x1 1.73 us: finish(): pl.pallas_call(finish_kernel, in_specs=[pl.BlockSpec(memory_space=pltpu.S...]
  transfers between devices with their start and end apart: 38 -> 38, of which waited for: 16 -> 17; matrix products, arithmetic and copies ran while one was open for 3% -> 0% of each run, Pallas kernels for 8% -> 3%
where the time goes in v3:
time: 230 us; the launch traced here: 229 us
  starting transfers between devices  110 us (48%)
  waiting for transfers between devices  48.4 us (21%)
  local copies, waits for them, and re-layouts  48.3 us (21%)
  Pallas kernels  16.3 us (7%)
  other arithmetic  4.03 us (2%)
    ppermute x38, starting transfers between devices, move(): return lax.ppermute(value, BOTH, pairs)  110 us
    ppermute x38, waiting for transfers between devices, move(): return lax.ppermute(value, BOTH, pairs)  48.4 us
    unnamed x108, local copies, waits for them, and re-layouts  48 us
    pallas_call x1, Pallas kernels, run_middle(): pl.pallas_call(middle_kernel, grid_spec=pltpu.PrefetchScalarGridSpec(num_...  7.36 us
    pallas_call x2, Pallas kernels, run_backward(): pl.pallas_call(functools.partial(backward_kernel, first, last), grid_spec...  5.28 us
  transfers between devices with their start and end apart: 38, of which 17 were waited for; matrix products, arithmetic and copies ran while one was open for 0% of the time, Pallas kernels for 3%

profile of v3, /device:TPU:1, one launch (start us, length us, event | category | flops | bytes accessed | tf_op | source)
XLA Modules:
  0.0 228.7 jit_solution(9969983494113163577)
XLA Ops:
  5.8 5.6 %collective-permute-start.3 = (bf16[48,2048]{1,0:T(8,128)(2,1)S(1)}, bf16[48,2048]{1,0:T(8,128)(2,1)S(1)}, u32[]{:S(2)}, u32[]{:S(2)}) collective-permute-start(bf16[48,2048]{1,0:T(8,128)(2,1)S(1)} %pack_attention_weights.1), channel_id=1, source_target_pairs={{48,0},{115,1},{50,2},{113,3},{52,4},{119,5},{54,6},{117,7},{56,8}... | collective-permute-start | bytes 589832 | tf_op jit(solution)/shard_map/ppermute | solution.py:547
  13.0 4.1 %collective-permute-start.1 = (bf16[48,2048]{1,0:T(8,128)(2,1)S(1)}, bf16[48,2048]{1,0:T(8,128)(2,1)S(1)}, u32[]{:S(2)}, u32[]{:S(2)}) collective-permute-start(bf16[48,2048]{1,0:T(8,128)(2,1)S(1)} %pack_attention_weights.1), channel_id=1, source_target_pairs={{16,0},{83,1},{18,2},{81,3},{20,4},{87,5},{22,6},{85,7},{24,8},{91... | collective-permute-start | bytes 589832 | tf_op jit(solution)/shard_map/ppermute | solution.py:547
  21.7 2.7 %collective-permute-done.1.p1 = bf16[48,2048]{1,0:T(8,128)(2,1)S(1)} collective-permute-done((bf16[48,2048]{1,0:T(8,128)(2,1)S(1)}, bf16[48,2048]{1,0:T(8,128)(2,1)S(1)}, u32[]{:S(2)}, u32[]{:S(2)}) %collective-permute-start.1) | collective-permute-done | bytes 196640 | tf_op jit(solution)/shard_map/ppermute | solution.py:547
  30.7 3.6 %collective-permute-start.10 = (bf16[48,5120]{1,0:T(8,128)(2,1)}, bf16[48,5120]{1,0:T(8,128)(2,1)}, u32[]{:S(2)}, u32[]{:S(2)}) collective-permute-start(bf16[48,5120]{1,0:T(8,128)(2,1)} %pack_feed_forward_weights.1), channel_id=1, source_target_pairs={{32,0},{99,1},{34,2},{97,3},{36,4},{103,5},{38,6},{101,7},{40,8},{... | collective-permute-start | bytes 1474568 | tf_op jit(solution)/shard_map/ppermute | solution.py:547
  37.0 4.4 %collective-permute-start.8 = (bf16[48,5120]{1,0:T(8,128)(2,1)}, bf16[48,5120]{1,0:T(8,128)(2,1)}, u32[]{:S(2)}, u32[]{:S(2)}) collective-permute-start(bf16[48,5120]{1,0:T(8,128)(2,1)} %pack_feed_forward_weights.1), channel_id=1, source_target_pairs={{0,0},{67,1},{2,2},{65,3},{4,4},{71,5},{6,6},{69,7},{8,8},{75,9},{... | collective-permute-start | bytes 1474568 | tf_op jit(solution)/shard_map/ppermute | solution.py:547
  54.0 2.6 %copy-done = bf16[8,6,256,256]{3,2,1,0:T(8,128)(2,1)} copy-done((bf16[8,6,256,256]{3,2,1,0:T(8,128)(2,1)}, bf16[8,6,256,256]{3,2,1,0:T(8,128)(2,1)S(1)}, u32[]{:S(2)}) %copy-start) | copy-done | bytes 6291480
  61.1 3.1 %collective-permute-start.12 = (bf16[48,5120]{1,0:T(8,128)(2,1)}, bf16[48,5120]{1,0:T(8,128)(2,1)S(1)}, u32[]{:S(2)}, u32[]{:S(2)}) collective-permute-start(bf16[48,5120]{1,0:T(8,128)(2,1)} %collective-permute-done.8.p0), channel_id=1, source_target_pairs={{0,1},{1,0},{2,3},{3,2},{4,5},{5,4},{6,7},{7,6},{8,9},{9,8},{10,11... | collective-permute-start | bytes 1474568 | tf_op jit(solution)/shard_map/ppermute | solution.py:547
  68.0 7.4 %feed_forward_both_ways.1 = (bf16[384,5120]{1,0:T(8,128)(2,1)S(1)}, bf16[8,256,384]{2,1,0:T(8,128)(2,1)}, f32[8,256,384]{2,1,0:T(8,128)S(1)}, bf16[8,256,384]{2,...) custom-call(s32[4]{0:T(128)S(1)} %pad_add_fusion.info, ...), custom_call_target="tpu_custom_call" | custom-call | flops 16000000000 | bytes 30000000 | tf_op jit(solution)/shard_map/feed_forward_both_ways/pallas_call | solution.py:443
  81.5 10.6 %collective-permute-start.16 = (bf16[192,5120]{1,0:T(8,128)(2,1)}, bf16[192,5120]{1,0:T(8,128)(2,1)}, u32[]{:S(2)}, u32[]{:S(2)}) collective-permute-start(bf16[192,5120]{1,0:T(8,128)(2,1)} %get-tuple-element.76), channel_id=1, source_target_pairs={{0,1},{1,0},{2,3},{3,2},{4,5},{5,4},{6,7},{7,6},{8,9},{9,8},{10,11... | collective-permute-start | bytes 5898248 | tf_op jit(solution)/shard_map/ppermute | solution.py:547
  92.1 2.8 %copy-done.1 = bf16[8,6,256,256]{3,2,1,0:T(8,128)(2,1)S(1)} copy-done((bf16[8,6,256,256]{3,2,1,0:T(8,128)(2,1)S(1)}, bf16[8,6,256,256]{3,2,1,0:T(8,128)(2,1)}, u32[]{:S(2)}) %copy-start.1) | copy-done | bytes 6291480
  107.7 3.0 %add_convert_fusion = bf16[192,5120]{1,0:T(8,128)(2,1)S(1)} fusion(bf16[192,5120]{1,0:T(8,128)(2,1)} %collective-permute-done.16, bf16[192,5120]{1,0:T(8,128)(2,1)S(1)} %copy-done.25), kind=kLoop, calls=%fused_computation | loop fusion | flops 3932160 | bytes 5898240 | tf_op jit(solution)/shard_map/convert_element_type | solution.py:567
  110.9 20.7 %collective-permute-start.20 = (bf16[48,5120]{1,0:T(8,128)(2,1)S(1)}, bf16[48,5120]{1,0:T(8,128)(2,1)S(1)}, u32[]{:S(2)}, u32[]{:S(2)}) collective-permute-start(bf16[48,5120]{1,0:T(8,128)(2,1)S(1)} %get-tuple-element.95), channel_id=1, source_target_pairs={{0,48},{1,115},{2,50},{3,113},{4,52},{5,119},{6,54},{7,117},{8,56}... | collective-permute-start | bytes 1474568 | tf_op jit(solution)/shard_map/ppermute | solution.py:547
  131.5 21.7 %collective-permute-start.19 = (bf16[48,5120]{1,0:T(8,128)(2,1)S(1)}, bf16[48,5120]{1,0:T(8,128)(2,1)S(1)}, u32[]{:S(2)}, u32[]{:S(2)}) collective-permute-start(bf16[48,5120]{1,0:T(8,128)(2,1)S(1)} %get-tuple-element.96), channel_id=1, source_target_pairs={{0,32},{1,99},{2,34},{3,97},{4,36},{5,103},{6,38},{7,101},{8,40},{... | collective-permute-start | bytes 1474568 | tf_op jit(solution)/shard_map/ppermute | solution.py:547
  153.2 2.9 %collective-permute-start.18 = (bf16[48,5120]{1,0:T(8,128)(2,1)S(1)}, bf16[48,5120]{1,0:T(8,128)(2,1)S(1)}, u32[]{:S(2)}, u32[]{:S(2)}) collective-permute-start(bf16[48,5120]{1,0:T(8,128)(2,1)S(1)} %get-tuple-element.97), channel_id=1, source_target_pairs={{0,16},{1,83},{2,18},{3,81},{4,20},{5,87},{6,22},{7,85},{8,24},{9,... | collective-permute-start | bytes 1474568 | tf_op jit(solution)/shard_map/ppermute | solution.py:547
  158.3 3.8 %attention_backward_rest.1 = (bf16[8,256,384]{2,1,0:T(8,128)(2,1)}, bf16[8,384]{1,0:T(8,128)(2,1)}, bf16[192,2048]{1,0:T(8,128)(2,1)S(1)}, bf16[192,2048]{1,0:T(8,128)(2,1)S(1)}) custom-call(s32[4]{0:T(128)S(1)} %pad_add_fusion.info, bf16[8,256,384]{2,1,0:T(8,128)(2,1)S(1)} %copy-done.11, ...), custom_call_target="tpu_custom_call", output_to_operand_aliasing={{0}: (17, {})} | custom-call | flops 6600000000 | bytes 24000000 | tf_op jit(solution)/shard_map/attention_backward_rest/pallas_call | solution.py:500
  164.1 11.1 %collective-permute-done.18 = bf16[48,5120]{1,0:T(8,128)(2,1)S(1)} collective-permute-done((bf16[48,5120]{1,0:T(8,128)(2,1)S(1)}, bf16[48,5120]{1,0:T(8,128)(2,1)S(1)}, u32[]{:S(2)}, u32[]{:S(2)}) %collective-permute-start.18) | collective-permute-done | bytes 491552 | tf_op jit(solution)/shard_map/ppermute | solution.py:547
  175.2 3.5 %collective-permute-start.21 = (bf16[192,2048]{1,0:T(8,128)(2,1)S(1)}, bf16[192,2048]{1,0:T(8,128)(2,1)S(1)}, u32[]{:S(2)}, u32[]{:S(2)}) collective-permute-start(bf16[192,2048]{1,0:T(8,128)(2,1)S(1)} %get-tuple-element.84), channel_id=1, source_target_pairs={{0,1},{1,0},{2,3},{3,2},{4,5},{5,4},{6,7},{7,6},{8,9},{9,8},{10,11... | collective-permute-start | bytes 2359304 | tf_op jit(solution)/shard_map/ppermute | solution.py:547
  180.9 4.4 %collective-permute-start.22 = (bf16[48,2048]{1,0:T(8,128)(2,1)S(1)}, bf16[48,2048]{1,0:T(8,128)(2,1)S(1)}, u32[]{:S(2)}, u32[]{:S(2)}) collective-permute-start(bf16[48,2048]{1,0:T(8,128)(2,1)S(1)} %get-tuple-element.99), channel_id=1, source_target_pairs={{0,0},{1,67},{2,2},{3,65},{4,4},{5,71},{6,6},{7,69},{8,8},{9,75},{... | collective-permute-start | bytes 589832 | tf_op jit(solution)/shard_map/ppermute | solution.py:547
  185.3 3.4 %collective-permute-start.25 = (bf16[48,2048]{1,0:T(8,128)(2,1)S(1)}, bf16[48,2048]{1,0:T(8,128)(2,1)S(1)}, u32[]{:S(2)}, u32[]{:S(2)}) collective-permute-start(bf16[48,2048]{1,0:T(8,128)(2,1)S(1)} %get-tuple-element.100), channel_id=1, source_target_pairs={{0,48},{1,115},{2,50},{3,113},{4,52},{5,119},{6,54},{7,117},{8,56}... | collective-permute-start | bytes 589832 | tf_op jit(solution)/shard_map/ppermute | solution.py:547
  189.5 5.1 %collective-permute-done.25 = bf16[48,2048]{1,0:T(8,128)(2,1)S(1)} collective-permute-done((bf16[48,2048]{1,0:T(8,128)(2,1)S(1)}, bf16[48,2048]{1,0:T(8,128)(2,1)S(1)}, u32[]{:S(2)}, u32[]{:S(2)}) %collective-permute-start.25) | collective-permute-done | bytes 196640 | tf_op jit(solution)/shard_map/ppermute | solution.py:547
  200.9 5.5 %collective-permute-done.33 = bf16[48,2560]{1,0:T(8,128)(2,1)S(1)} collective-permute-done((bf16[48,2560]{1,0:T(8,128)(2,1)S(1)}, bf16[48,2560]{1,0:T(8,128)(2,1)S(1)}, u32[]{:S(2)}, u32[]{:S(2)}) %collective-permute-start.33) | collective-permute-done | bytes 245792 | tf_op jit(solution)/shard_map/ppermute | solution.py:547
  206.5 2.6 %collective-permute-start.35 = (bf16[48,2560]{1,0:T(8,128)(2,1)S(1)}, bf16[48,2560]{1,0:T(8,128)(2,1)S(1)}, u32[]{:S(2)}, u32[]{:S(2)}) collective-permute-start(bf16[48,2560]{1,0:T(8,128)(2,1)S(1)} %add_convert_fusion.4), channel_id=1, source_target_pairs={{0,8},{1,9},{2,10},{3,11},{4,12},{5,13},{6,14},{7,15},{8,0},{9,1},... | collective-permute-start | bytes 737288 | tf_op jit(solution)/shard_map/ppermute | solution.py:547
  213.1 7.8 %collective-permute-done.34 = bf16[48,2560]{1,0:T(8,128)(2,1)S(1)} collective-permute-done((bf16[48,2560]{1,0:T(8,128)(2,1)S(1)}, bf16[48,2560]{1,0:T(8,128)(2,1)S(1)}, u32[]{:S(2)}, u32[]{:S(2)}) %collective-permute-start.34) | collective-permute-done | bytes 245792 | tf_op jit(solution)/shard_map/ppermute | solution.py:547
  221.0 3.0 %collective-permute-start.37 = (bf16[48,2560]{1,0:T(8,128)(2,1)S(1)}, bf16[48,2560]{1,0:T(8,128)(2,1)S(1)}, u32[]{:S(2)}, u32[]{:S(2)}) collective-permute-start(bf16[48,2560]{1,0:T(8,128)(2,1)S(1)} %add_convert_fusion.3.two_a), channel_id=1, source_target_pairs={{0,1},{1,0},{2,3},{3,2},{4,5},{5,4},{6,7},{7,6},{8,9},{9,8},{10,11... | collective-permute-start | bytes 737288 | tf_op jit(solution)/shard_map/ppermute | solution.py:547
  (182 shorter events, 82.1 us)
Async XLA Ops:
  5.8 13.2 %collective-permute-start.3 = (bf16[48,2048]{1,0:T(8,128)(2,1)S(1)}, bf16[48,2048]{1,0:T(8,128)(2,1)S(1)}, u32[]{:S(2)}, u32[]{:S(2)}) collective-permute-start(bf16[48,2048]{1,0:T(8,128)(2,1)S(1)} %pack_attention_weights.1), channel_id=1, source_target_pairs={{48,0},{115,1},{50,2},{113,3},{52,4},{119,5},{54,6},{117,7},{56,8}... | collective-permute-start | bytes 589832 | tf_op jit(solution)/shard_map/ppermute | solution.py:547
  11.4 10.3 %collective-permute-start.2 = (bf16[48,2048]{1,0:T(8,128)(2,1)S(1)}, bf16[48,2048]{1,0:T(8,128)(2,1)S(1)}, u32[]{:S(2)}, u32[]{:S(2)}) collective-permute-start(bf16[48,2048]{1,0:T(8,128)(2,1)S(1)} %pack_attention_weights.1), channel_id=1, source_target_pairs={{32,0},{99,1},{34,2},{97,3},{36,4},{103,5},{38,6},{101,7},{40,8},{... | collective-permute-start | bytes 589832 | tf_op jit(solution)/shard_map/ppermute | solution.py:547
  13.0 11.4 %collective-permute-start.1 = (bf16[48,2048]{1,0:T(8,128)(2,1)S(1)}, bf16[48,2048]{1,0:T(8,128)(2,1)S(1)}, u32[]{:S(2)}, u32[]{:S(2)}) collective-permute-start(bf16[48,2048]{1,0:T(8,128)(2,1)S(1)} %pack_attention_weights.1), channel_id=1, source_target_pairs={{16,0},{83,1},{18,2},{81,3},{20,4},{87,5},{22,6},{85,7},{24,8},{91... | collective-permute-start | bytes 589832 | tf_op jit(solution)/shard_map/ppermute | solution.py:547
  17.1 11.7 %collective-permute-start = (bf16[48,2048]{1,0:T(8,128)(2,1)S(1)}, bf16[48,2048]{1,0:T(8,128)(2,1)S(1)}, u32[]{:S(2)}, u32[]{:S(2)}) collective-permute-start(bf16[48,2048]{1,0:T(8,128)(2,1)S(1)} %pack_attention_weights.1), channel_id=1, source_target_pairs={{0,0},{67,1},{2,2},{65,3},{4,4},{71,5},{6,6},{69,7},{8,8},{75,9},{... | collective-permute-start | bytes 589832 | tf_op jit(solution)/shard_map/ppermute | solution.py:547
  19.0 15.2 %collective-permute-start.7 = (bf16[48,2048]{1,0:T(8,128)(2,1)S(1)}, bf16[48,2048]{1,0:T(8,128)(2,1)S(1)}, u32[]{:S(2)}, u32[]{:S(2)}) collective-permute-start(bf16[48,2048]{1,0:T(8,128)(2,1)S(1)} %collective-permute-done.3.p3), channel_id=1, source_target_pairs={{0,1},{1,0},{2,3},{3,2},{4,5},{5,4},{6,7},{7,6},{8,9},{9,8},{10,11... | collective-permute-start | bytes 589832 | tf_op jit(solution)/shard_map/ppermute | solution.py:547
  21.7 14.6 %collective-permute-start.6 = (bf16[48,2048]{1,0:T(8,128)(2,1)S(1)}, bf16[48,2048]{1,0:T(8,128)(2,1)S(1)}, u32[]{:S(2)}, u32[]{:S(2)}) collective-permute-start(bf16[48,2048]{1,0:T(8,128)(2,1)S(1)} %collective-permute-done.2.p2), channel_id=1, source_target_pairs={{0,1},{1,0},{2,3},{3,2},{4,5},{5,4},{6,7},{7,6},{8,9},{9,8},{10,11... | collective-permute-start | bytes 589832 | tf_op jit(solution)/shard_map/ppermute | solution.py:547
  24.4 17.0 %collective-permute-start.5 = (bf16[48,2048]{1,0:T(8,128)(2,1)S(1)}, bf16[48,2048]{1,0:T(8,128)(2,1)S(1)}, u32[]{:S(2)}, u32[]{:S(2)}) collective-permute-start(bf16[48,2048]{1,0:T(8,128)(2,1)S(1)} %collective-permute-done.1.p1), channel_id=1, source_target_pairs={{0,1},{1,0},{2,3},{3,2},{4,5},{5,4},{6,7},{7,6},{8,9},{9,8},{10,11... | collective-permute-start | bytes 589832 | tf_op jit(solution)/shard_map/ppermute | solution.py:547
  28.8 32.3 %collective-permute-start.11 = (bf16[48,5120]{1,0:T(8,128)(2,1)}, bf16[48,5120]{1,0:T(8,128)(2,1)}, u32[]{:S(2)}, u32[]{:S(2)}) collective-permute-start(bf16[48,5120]{1,0:T(8,128)(2,1)} %pack_feed_forward_weights.1), channel_id=1, source_target_pairs={{48,0},{115,1},{50,2},{113,3},{52,4},{119,5},{54,6},{117,7},{56,8}... | collective-permute-start | bytes 1474568 | tf_op jit(solution)/shard_map/ppermute | solution.py:547
  30.7 30.4 %collective-permute-start.10 = (bf16[48,5120]{1,0:T(8,128)(2,1)}, bf16[48,5120]{1,0:T(8,128)(2,1)}, u32[]{:S(2)}, u32[]{:S(2)}) collective-permute-start(bf16[48,5120]{1,0:T(8,128)(2,1)} %pack_feed_forward_weights.1), channel_id=1, source_target_pairs={{32,0},{99,1},{34,2},{97,3},{36,4},{103,5},{38,6},{101,7},{40,8},{... | collective-permute-start | bytes 1474568 | tf_op jit(solution)/shard_map/ppermute | solution.py:547
  35.0 26.1 %collective-permute-start.9 = (bf16[48,5120]{1,0:T(8,128)(2,1)}, bf16[48,5120]{1,0:T(8,128)(2,1)}, u32[]{:S(2)}, u32[]{:S(2)}) collective-permute-start(bf16[48,5120]{1,0:T(8,128)(2,1)} %pack_feed_forward_weights.1), channel_id=1, source_target_pairs={{16,0},{83,1},{18,2},{81,3},{20,4},{87,5},{22,6},{85,7},{24,8},{91... | collective-permute-start | bytes 1474568 | tf_op jit(solution)/shard_map/ppermute | solution.py:547
  37.0 24.1 %collective-permute-start.8 = (bf16[48,5120]{1,0:T(8,128)(2,1)}, bf16[48,5120]{1,0:T(8,128)(2,1)}, u32[]{:S(2)}, u32[]{:S(2)}) collective-permute-start(bf16[48,5120]{1,0:T(8,128)(2,1)} %pack_feed_forward_weights.1), channel_id=1, source_target_pairs={{0,0},{67,1},{2,2},{65,3},{4,4},{71,5},{6,6},{69,7},{8,8},{75,9},{... | collective-permute-start | bytes 1474568 | tf_op jit(solution)/shard_map/ppermute | solution.py:547
  81.5 26.1 %collective-permute-start.16 = (bf16[192,5120]{1,0:T(8,128)(2,1)}, bf16[192,5120]{1,0:T(8,128)(2,1)}, u32[]{:S(2)}, u32[]{:S(2)}) collective-permute-start(bf16[192,5120]{1,0:T(8,128)(2,1)} %get-tuple-element.76), channel_id=1, source_target_pairs={{0,1},{1,0},{2,3},{3,2},{4,5},{5,4},{6,7},{7,6},{8,9},{9,8},{10,11... | collective-permute-start | bytes 5898248 | tf_op jit(solution)/shard_map/ppermute | solution.py:547
  110.9 51.2 %collective-permute-start.20 = (bf16[48,5120]{1,0:T(8,128)(2,1)S(1)}, bf16[48,5120]{1,0:T(8,128)(2,1)S(1)}, u32[]{:S(2)}, u32[]{:S(2)}) collective-permute-start(bf16[48,5120]{1,0:T(8,128)(2,1)S(1)} %get-tuple-element.95), channel_id=1, source_target_pairs={{0,48},{1,115},{2,50},{3,113},{4,52},{5,119},{6,54},{7,117},{8,56}... | collective-permute-start | bytes 1474568 | tf_op jit(solution)/shard_map/ppermute | solution.py:547
  131.5 32.6 %collective-permute-start.19 = (bf16[48,5120]{1,0:T(8,128)(2,1)S(1)}, bf16[48,5120]{1,0:T(8,128)(2,1)S(1)}, u32[]{:S(2)}, u32[]{:S(2)}) collective-permute-start(bf16[48,5120]{1,0:T(8,128)(2,1)S(1)} %get-tuple-element.96), channel_id=1, source_target_pairs={{0,32},{1,99},{2,34},{3,97},{4,36},{5,103},{6,38},{7,101},{8,40},{... | collective-permute-start | bytes 1474568 | tf_op jit(solution)/shard_map/ppermute | solution.py:547
  153.2 22.0 %collective-permute-start.18 = (bf16[48,5120]{1,0:T(8,128)(2,1)S(1)}, bf16[48,5120]{1,0:T(8,128)(2,1)S(1)}, u32[]{:S(2)}, u32[]{:S(2)}) collective-permute-start(bf16[48,5120]{1,0:T(8,128)(2,1)S(1)} %get-tuple-element.97), channel_id=1, source_target_pairs={{0,16},{1,83},{2,18},{3,81},{4,20},{5,87},{6,22},{7,85},{8,24},{9,... | collective-permute-start | bytes 1474568 | tf_op jit(solution)/shard_map/ppermute | solution.py:547
  156.1 19.1 %collective-permute-start.17 = (bf16[48,5120]{1,0:T(8,128)(2,1)S(1)}, bf16[48,5120]{1,0:T(8,128)(2,1)S(1)}, u32[]{:S(2)}, u32[]{:S(2)}) collective-permute-start(bf16[48,5120]{1,0:T(8,128)(2,1)S(1)} %get-tuple-element.98), channel_id=1, source_target_pairs={{0,0},{1,67},{2,2},{3,65},{4,4},{5,71},{6,6},{7,69},{8,8},{9,75},{... | collective-permute-start | bytes 1474568 | tf_op jit(solution)/shard_map/ppermute | solution.py:547
  185.3 9.3 %collective-permute-start.25 = (bf16[48,2048]{1,0:T(8,128)(2,1)S(1)}, bf16[48,2048]{1,0:T(8,128)(2,1)S(1)}, u32[]{:S(2)}, u32[]{:S(2)}) collective-permute-start(bf16[48,2048]{1,0:T(8,128)(2,1)S(1)} %get-tuple-element.100), channel_id=1, source_target_pairs={{0,48},{1,115},{2,50},{3,113},{4,52},{5,119},{6,54},{7,117},{8,56}... | collective-permute-start | bytes 589832 | tf_op jit(solution)/shard_map/ppermute | solution.py:547
  189.4 9.5 %collective-permute-start.23 = (bf16[48,2048]{1,0:T(8,128)(2,1)S(1)}, bf16[48,2048]{1,0:T(8,128)(2,1)S(1)}, u32[]{:S(2)}, u32[]{:S(2)}) collective-permute-start(bf16[48,2048]{1,0:T(8,128)(2,1)S(1)} %get-tuple-element.102), channel_id=1, source_target_pairs={{0,16},{1,83},{2,18},{3,81},{4,20},{5,87},{6,22},{7,85},{8,24},{9,... | collective-permute-start | bytes 589832 | tf_op jit(solution)/shard_map/ppermute | solution.py:547
  189.4 9.7 %collective-permute-start.32 = (bf16[48,2560]{1,0:T(8,128)(2,1)S(1)}, bf16[48,2560]{1,0:T(8,128)(2,1)S(1)}, u32[]{:S(2)}, u32[]{:S(2)}) collective-permute-start(bf16[48,2560]{1,0:T(8,128)(2,1)S(1)} %constant_dynamic-slice_fusion), channel_id=1, source_target_pairs={{0,1},{1,0},{2,3},{3,2},{4,5},{5,4},{6,7},{7,6},{8,9},{9,8},{10,11... | collective-permute-start | bytes 737288 | tf_op jit(solution)/shard_map/ppermute | solution.py:547
  200.4 9.4 %collective-permute-start.27 = (bf16[48,1024]{1,0:T(8,128)(2,1)S(1)}, bf16[48,1024]{1,0:T(8,128)(2,1)S(1)}, u32[]{:S(2)}, u32[]{:S(2)}) collective-permute-start(bf16[48,1024]{1,0:T(8,128)(2,1)S(1)} %add_convert_fusion.9), channel_id=1, source_target_pairs={{0,2},{1,3},{2,0},{3,1},{4,6},{5,7},{6,4},{7,5},{8,10},{9,11},{10,... | collective-permute-start | bytes 294920 | tf_op jit(solution)/shard_map/ppermute | solution.py:547
  209.1 11.8 %collective-permute-start.34 = (bf16[48,2560]{1,0:T(8,128)(2,1)S(1)}, bf16[48,2560]{1,0:T(8,128)(2,1)S(1)}, u32[]{:S(2)}, u32[]{:S(2)}) collective-permute-start(bf16[48,2560]{1,0:T(8,128)(2,1)S(1)} %add_convert_fusion.4), channel_id=1, source_target_pairs={{0,4},{1,5},{2,6},{3,7},{4,8},{5,9},{6,10},{7,11},{8,12},{9,13},{1... | collective-permute-start | bytes 737288 | tf_op jit(solution)/shard_map/ppermute | solution.py:547
  209.9 14.1 %collective-permute-start.30 = (bf16[48,1024]{1,0:T(8,128)(2,1)S(1)}, bf16[48,1024]{1,0:T(8,128)(2,1)S(1)}, u32[]{:S(2)}, u32[]{:S(2)}) collective-permute-start(bf16[48,1024]{1,0:T(8,128)(2,1)S(1)} %add_convert_fusion.8), channel_id=1, source_target_pairs={{0,12},{1,13},{2,14},{3,15},{4,0},{5,1},{6,2},{7,3},{8,4},{9,5},{1... | collective-permute-start | bytes 294920 | tf_op jit(solution)/shard_map/ppermute | solution.py:547
  211.9 12.1 %collective-permute-start.29 = (bf16[48,1024]{1,0:T(8,128)(2,1)S(1)}, bf16[48,1024]{1,0:T(8,128)(2,1)S(1)}, u32[]{:S(2)}, u32[]{:S(2)}) collective-permute-start(bf16[48,1024]{1,0:T(8,128)(2,1)S(1)} %add_convert_fusion.8), channel_id=1, source_target_pairs={{0,8},{1,9},{2,10},{3,11},{4,12},{5,13},{6,14},{7,15},{8,0},{9,1},... | collective-permute-start | bytes 294920 | tf_op jit(solution)/shard_map/ppermute | solution.py:547
  211.9 12.1 %collective-permute-start.28 = (bf16[48,1024]{1,0:T(8,128)(2,1)S(1)}, bf16[48,1024]{1,0:T(8,128)(2,1)S(1)}, u32[]{:S(2)}, u32[]{:S(2)}) collective-permute-start(bf16[48,1024]{1,0:T(8,128)(2,1)S(1)} %add_convert_fusion.8), channel_id=1, source_target_pairs={{0,4},{1,5},{2,6},{3,7},{4,8},{5,9},{6,10},{7,11},{8,12},{9,13},{1... | collective-permute-start | bytes 294920 | tf_op jit(solution)/shard_map/ppermute | solution.py:547
  (68 other events, 501.5 us)
